TPU v7x, 32 devices: a whole 2x2x4 slice. The times are simulated.
32 devices in a mesh: groups: 2 (over x), lat: 4 (over y, core), lon: 4 (over z).
Axes of the slice: x: 2, y: 2, z: 4, core: 2. Of those that a mesh axis runs over, the one named last changes fastest.
Arguments:
- fields: bfloat16 [256, 160, 69], P(('groups', 'lat'), 'lon'), parts along dimension 0, may hold values from -6 to 6
- first_kernel: bfloat16 [3, 3, 69, 256], replicated, may hold values from -0.25 to 0.25
- second_kernel: bfloat16 [3, 3, 256, 256], replicated, may hold values from -0.125 to 0.125
- down_weight: bfloat16 [4096, 1024], P(('lat', 'lon')), may hold values from -0.09375 to 0.09375
- projections: bfloat16 [1024, 3, 1024], replicated, may hold values from -0.1875 to 0.1875
- output_weight: bfloat16 [1024, 1024], replicated, may hold values from -0.1875 to 0.1875
Outputs:
- latent: bfloat16 [64, 40, 1024], P(('groups', 'lat', 'lon')), parts along dimension 0
There are 2 independent parts, one for each index of `groups`. A program takes and returns all parts, laid end to end along the dimension named above; an argument that names none is the same for every part. Nothing has to cross between parts.
All inputs are finite; a program needn't handle non-finite values.
Results may differ from a plain program's by a relative error of at most 0.013.
Values may be sent and summed in bfloat16 or wider, within the bound.
A program may use at most 64 MiB of HBM per device.

v0:
```python
import jax
import jax.numpy as jnp
from jax import lax
from jax.sharding import PartitionSpec as P

C = 256
D = 1024
HD = 64


epsilon = 1e-05


def extended(cells, sides, width, closed):
    for axis, dim in sides:
        count = lax.axis_size(axis)
        ends = count if closed else count - 1
        head = lax.slice_in_dim(cells, 0, width, axis=dim)
        tail = lax.slice_in_dim(cells, cells.shape[dim] - width, cells.shape[dim], axis=dim)
        cells = jnp.concatenate(
            [
                lax.ppermute(tail, axis, [(i, (i + 1) % count) for i in range(ends)]),
                cells,
                lax.ppermute(head, axis, [((i + 1) % count, i) for i in range(ends)]),
            ],
            axis=dim,
        )
    return cells


def extend(field, margin):
    wider = extended(field, (("lat", 0),), margin, False)
    return extended(wider, (("lon", 1),), margin, True)


def convolve_tile(padded, kernel, row_count, col_count):
    total = jnp.zeros((row_count * col_count, kernel.shape[3]), jnp.float32)
    for row_shift in range(3):
        for col_shift in range(3):
            window = padded[
                row_shift : row_shift + row_count, col_shift : col_shift + col_count
            ].reshape(row_count * col_count, -1)
            total = total + jnp.dot(
                window, kernel[row_shift, col_shift], preferred_element_type=jnp.float32
            )
    return total.reshape(row_count, col_count, -1)


def attention(band, query_weight, key_weight, value_weight):
    row_count, token_count = (band.shape[0], band.shape[1])
    widened = band.astype(jnp.float32)
    average = jnp.mean(widened, axis=-1, keepdims=True)
    centred = widened - average
    spread = jnp.mean(centred * centred, axis=-1, keepdims=True)
    normed = (
        (centred * lax.rsqrt(spread + epsilon))
        .astype(jnp.bfloat16)
        .reshape(row_count * token_count, -1)
    )
    head_count = query_weight.shape[1] // HD

    def project(weight):
        return (
            jnp.dot(normed, weight, preferred_element_type=jnp.float32)
            .astype(jnp.bfloat16)
            .reshape(row_count, token_count, head_count, HD)
        )

    query = project(query_weight)
    keys = project(key_weight)
    values = project(value_weight)
    scores = jnp.einsum(
        "rqhd,rkhd->rhqk", query, keys, preferred_element_type=jnp.float32
    ) * HD ** (-0.5)
    probs = jax.nn.softmax(scores, axis=-1).astype(jnp.bfloat16)
    mixed = jnp.einsum("rhqk,rkhd->rqhd", probs, values, preferred_element_type=jnp.float32).astype(
        jnp.bfloat16
    )
    return mixed.reshape(row_count * token_count, head_count * HD)


def on_device(fields, first_kernel, second_kernel, down_weight, projections, output_weight):
    row_count, col_count = (fields.shape[0], fields.shape[1])
    first = jax.nn.gelu(
        convolve_tile(extend(fields, 1), first_kernel, row_count, col_count)
    ).astype(jnp.bfloat16)
    middle = convolve_tile(extend(first, 1), second_kernel, row_count, col_count)
    second = (first.astype(jnp.float32) + jax.nn.gelu(middle)).astype(jnp.bfloat16)
    token_rows, token_cols = (row_count // 4, col_count // 4)
    patches = (
        second.reshape(token_rows, 4, token_cols, 4, C)
        .transpose(0, 2, 1, 3, 4)
        .reshape(token_rows * token_cols, 16 * C)
    )
    tokens = jnp.dot(
        patches,
        lax.all_gather(down_weight, ("lat", "lon"), axis=0, tiled=True),
        preferred_element_type=jnp.float32,
    )
    tokens = tokens.astype(jnp.bfloat16).reshape(token_rows, token_cols, D)
    band = lax.all_to_all(tokens, "lon", split_axis=0, concat_axis=1, tiled=True)
    mixed = attention(band, projections[:, 0], projections[:, 1], projections[:, 2])
    summed = band.astype(jnp.float32).reshape(-1, D) + jnp.dot(
        mixed, output_weight, preferred_element_type=jnp.float32
    )
    return summed.astype(jnp.bfloat16).reshape(band.shape)


def solution(mesh):
    placed = (P(("groups", "lat"), "lon", None), P(), P(), P(("lat", "lon"), None), P(), P())
    return jax.shard_map(
        on_device,
        mesh=mesh,
        in_specs=placed,
        out_specs=P(("groups", "lat", "lon"), None, None),
        check_vma=False,
    )
```

profile of v0, /device:TPU:0, one launch (start us, length us, event | category | flops | bytes accessed | tf_op | source)
XLA Modules:
  0.0 124.1 jit_solution(3568162317458559649)
XLA Ops:
  6.5 0.7 all-gather.2.cloned.1.call-update
  7.3 0.7 fusion.129
  8.0 2.3 %collective-permute-start = (bf16[1,40,69]{2,1,0:T(8,128)(2,1)S(1)}, bf16[1,40,69]{2,1,0:T(8,128)(2,1)S(1)}, u32[]{:S(2)}, u32[]{:S(2)}) collective-permute-start(bf16[1,40,69]{2,1,0:T(8,128)(2,1)S(1)} %get-tuple-element.34), channel_id=1, source_target_pairs={{0,4},{4,8},{8,12},{1,5},{5,9},{9,13},{2,6},{6,10},{10,14},{3,7},{... | collective-permute-start | bytes 16568 | tf_op jit(solution)/shard_map/ppermute | solution.py:22
  10.3 1.3 %collective-permute-start.1 = (bf16[1,40,69]{2,1,0:T(8,128)(2,1)S(1)}, bf16[1,40,69]{2,1,0:T(8,128)(2,1)S(1)}, u32[]{:S(2)}, u32[]{:S(2)}) collective-permute-start(bf16[1,40,69]{2,1,0:T(8,128)(2,1)S(1)} %get-tuple-element.33), channel_id=1, source_target_pairs={{4,0},{8,4},{12,8},{5,1},{9,5},{13,9},{6,2},{10,6},{14,10},{7,3},{... | collective-permute-start | bytes 16568 | tf_op jit(solution)/shard_map/ppermute | solution.py:24
  11.7 3.9 %collective-permute-done.1 = bf16[1,40,69]{2,1,0:T(8,128)(2,1)S(1)} collective-permute-done((bf16[1,40,69]{2,1,0:T(8,128)(2,1)S(1)}, bf16[1,40,69]{2,1,0:T(8,128)(2,1)S(1)}, u32[]{:S(2)}, u32[]{:S(2)}) %collective-permute-start.1) | collective-permute-done | bytes 5552 | tf_op jit(solution)/shard_map/ppermute | solution.py:24
  15.5 1.4 %pad_maximum_fusion.6 = (bf16[32,40,69]{2,1,0:T(8,128)(2,1)S(1)}, bf16[32,40,69]{2,1,0:T(8,128)(2,1)S(1)}, bf16[34,40,69]{2,1,0:T(8,128)(2,1)S(1)}) fusion(bf16[32,40,69]{2,1,0:T(8,128)(2,1)} %param.6, bf16[1,40,69]{2,1,0:T(8,128)(2,1)S(1)} %collective-permute-done, bf16[1,40,69]{2,1,0:T(8,128)(2,1)S(1)} %collective-permute-done.1, ...), kind=kLoop, calls=%fused_computation.102 | loop fusion | flops 706560 | bytes 1180160 | tf_op jit(solution)/shard_map/concatenate | solution.py:20
  17.0 1.6 %collective-permute-start.2 = (bf16[34,1,69]{2,1,0:T(2,128)(2,1)S(1)}, bf16[34,1,69]{2,1,0:T(2,128)(2,1)S(1)}, u32[]{:S(2)}, u32[]{:S(2)}) collective-permute-start(bf16[34,1,69]{2,1,0:T(2,128)(2,1)S(1)} %get-tuple-element.28), channel_id=1, source_target_pairs={{0,1},{1,2},{2,3},{3,0},{4,5},{5,6},{6,7},{7,4},{8,9},{9,10},{10,1... | collective-permute-start | bytes 14084 | tf_op jit(solution)/shard_map/ppermute | solution.py:22
  18.6 2.2 %collective-permute-start.3 = (bf16[34,1,69]{2,1,0:T(2,128)(2,1)S(1)}, bf16[34,1,69]{2,1,0:T(2,128)(2,1)S(1)}, u32[]{:S(2)}, u32[]{:S(2)}) collective-permute-start(bf16[34,1,69]{2,1,0:T(2,128)(2,1)S(1)} %get-tuple-element.29), channel_id=1, source_target_pairs={{1,0},{2,1},{3,2},{0,3},{5,4},{6,5},{7,6},{4,7},{9,8},{10,9},{11,1... | collective-permute-start | bytes 14084 | tf_op jit(solution)/shard_map/ppermute | solution.py:24
  20.9 0.3 fusion.102
  21.2 0.3 fusion.95
  21.5 1.1 collective-permute-done.2
  22.6 0.5 pad_maximum_fusion.5
  23.1 0.3 fusion.93
  23.4 0.3 convolution_add_fusion.12
  23.7 0.3 convolution_add_fusion.11
  24.0 0.3 convolution_add_fusion.10
  24.3 0.6 copy-done.4
  25.0 0.3 convolution_add_fusion.9
  25.3 0.3 convolution_add_fusion.8
  25.6 1.2 fusion.2
  26.8 0.4 fusion.29
  27.2 0.8 copy-done.1
  28.0 3.3 %collective-permute-start.4 = (bf16[1,40,256]{2,1,0:T(8,128)(2,1)S(1)}, bf16[1,40,256]{2,1,0:T(8,128)(2,1)S(1)}, u32[]{:S(2)}, u32[]{:S(2)}) collective-permute-start(bf16[1,40,256]{2,1,0:T(8,128)(2,1)S(1)} %get-tuple-element.17), channel_id=1, source_target_pairs={{0,4},{4,8},{8,12},{1,5},{5,9},{9,13},{2,6},{6,10},{10,14},{3,7},{... | collective-permute-start | bytes 61448 | tf_op jit(solution)/shard_map/ppermute | solution.py:22
  31.4 1.3 %collective-permute-start.5 = (bf16[1,40,256]{2,1,0:T(8,128)(2,1)S(1)}, bf16[1,40,256]{2,1,0:T(8,128)(2,1)S(1)}, u32[]{:S(2)}, u32[]{:S(2)}) collective-permute-start(bf16[1,40,256]{2,1,0:T(8,128)(2,1)S(1)} %get-tuple-element.18), channel_id=1, source_target_pairs={{4,0},{8,4},{12,8},{5,1},{9,5},{13,9},{6,2},{10,6},{14,10},{7,3},{... | collective-permute-start | bytes 61448 | tf_op jit(solution)/shard_map/ppermute | solution.py:24
  32.7 1.5 %reshape.162 = f32[8,4,10,4,256]{4,3,2,1,0:T(4,128)} reshape(f32[1280,256]{1,0:T(8,128)S(1)} %fusion.2) | data formatting | bytes 2621440 | tf_op jit(solution)/shard_map/reshape | solution.py:46
  34.2 0.8 collective-permute-done.5
  35.0 1.0 pad_maximum_fusion.9
  36.0 1.4 %collective-permute-start.6 = (bf16[34,1,256]{2,1,0:T(2,128)(2,1)S(1)}, bf16[34,1,256]{2,1,0:T(2,128)(2,1)S(1)}, u32[]{:S(2)}, u32[]{:S(2)}) collective-permute-start(bf16[34,1,256]{2,1,0:T(2,128)(2,1)S(1)} %get-tuple-element.13), channel_id=1, source_target_pairs={{0,1},{1,2},{2,3},{3,0},{4,5},{5,6},{6,7},{7,4},{8,9},{9,10},{10,1... | collective-permute-start | bytes 52232 | tf_op jit(solution)/shard_map/ppermute | solution.py:22
  37.4 2.9 %collective-permute-start.7 = (bf16[34,1,256]{2,1,0:T(2,128)(2,1)S(1)}, bf16[34,1,256]{2,1,0:T(2,128)(2,1)S(1)}, u32[]{:S(2)}, u32[]{:S(2)}) collective-permute-start(bf16[34,1,256]{2,1,0:T(2,128)(2,1)S(1)} %get-tuple-element.14), channel_id=1, source_target_pairs={{1,0},{2,1},{3,2},{0,3},{5,4},{6,5},{7,6},{4,7},{9,8},{10,9},{11,1... | collective-permute-start | bytes 52232 | tf_op jit(solution)/shard_map/ppermute | solution.py:24
  40.3 1.4 %pad_maximum_fusion.1 = (bf16[32,40,256]{2,1,0:T(8,128)(2,1)S(1)}, bf16[32,40,256]{2,1,0:T(8,128)(2,1)S(1)}) fusion(bf16[1,40,256]{2,1,0:T(8,128)(2,1)S(1)} %collective-permute-done.5, bf16[32,40,256]{2,1,0:T(8,128)(2,1)} %copy-done.1, bf16[1,40,256]{2,1,0:T(8,128)(2,1)S(1)} %collective-permute-done.4), kind=kLoop, calls=%fused_computation.76 | loop fusion | flops 655360 | bytes 2007040 | tf_op jit(solution)/shard_map/concatenate | solution.py:20
  41.7 0.3 fusion.81
  42.0 0.7 collective-permute-done.6
  42.8 0.5 maximum_maximum_fusion
  43.3 0.4 fusion.125
  43.7 0.3 fusion.73
  44.1 0.3 convolution_add_fusion.6
  44.4 0.3 convolution_add_fusion.5
  44.7 0.3 convolution_add_fusion.4
  45.1 0.6 convolution_add_fusion.3
  45.7 0.3 convolution_add_fusion.2
  46.0 0.3 convolution_add_fusion.1
  46.4 1.4 %fusion.3 = f32[1280,256]{1,0:T(8,128)} fusion(f32[1280,256]{1,0:T(8,128)S(1)} %fusion.73, f32[1280,256]{1,0:T(8,128)S(1)} %convolution_add_fusion.1, bf16[1280,256]{1,0:T(8,128)(2,1)S(1)} %bitcast.133, bf16[3,3,256,256]{3,2,1,0:T(8,128)(2,1)S(1)} %copy-done.5), kind=kOutput, calls=%fused_computation.16 | convolution fusion | flops 168427520 | bytes 4718592 | tf_op jit(solution)/shard_map/dot_general | solution.py:43
  47.7 2.7 %reshape.172 = f32[8,4,10,4,256]{4,3,2,1,0:T(4,128)} reshape(f32[1280,256]{1,0:T(8,128)} %fusion.3) | data formatting | bytes 2621440 | tf_op jit(solution)/shard_map/reshape | solution.py:46
  50.5 3.2 %fusion.64 = bf16[8,10,4,4,256]{4,0,3,1,2:T(8,128)(2,1)S(1)} fusion(f32[8,4,10,4,256]{4,3,2,1,0:T(4,128)} %reshape.172, f32[8,4,10,4,256]{4,3,2,1,0:T(4,128)S(1)} %copy-done.3), kind=kLoop, calls=%fused_computation.83 | loop fusion | flops 6553600 | bytes 3276800 | tf_op jit(solution)/shard_map/transpose | solution.py:92
  53.7 0.3 copy.45
  53.9 0.5 reshape.173
  54.4 33.4 %all-gather.2.cloned.1.call-done = bf16[4096,1024]{1,0:T(8,128)(2,1)} async-done(((bf16[256,1024]{1,0:T(8,128)(2,1)}), bf16[4096,1024]{1,0:T(8,128)(2,1)}) %all-gather.2.cloned.1.call-update) | async-done | bytes 8388624 | tf_op jit(solution)/shard_map/all_gather | solution.py:97
  87.8 4.9 %convolution_convert_fusion.1 = bf16[80,1024]{1,0:T(8,128)(2,1)S(1)} fusion(bf16[80,4096]{1,0:T(8,128)(2,1)S(1)} %reshape.173, bf16[4096,1024]{1,0:T(8,128)(2,1)} %all-gather.2.cloned.1.call-done), kind=kOutput, calls=%fused_computation.70 | convolution fusion | flops 671170560 | bytes 9207808 | tf_op jit(solution)/shard_map/dot_general | solution.py:95
  92.8 12.0 %all_to_all.4 = bf16[8,10,1024]{2,1,0:T(8,128)(2,1)S(1)} all-to-all(bf16[8,10,1024]{2,1,0:T(8,128)(2,1)S(1)} %reshape.174), channel_id=1, replica_groups=mesh['groups'=2,'lat'=4,'lon'=4] {'lon'}, dimensions={0} | all-to-all | bytes 327680 | tf_op jit(solution)/shard_map/all_to_all | solution.py:101
  104.9 0.1 fusion.124
  105.0 0.2 multiply_reduce_fusion
  105.2 0.2 multiply_convert_fusion
  105.4 0.1 convert_element_type.86
  105.5 2.1 %fusion.53 = bf16[80,1024]{1,0:T(8,128)(2,1)S(1)} fusion(bf16[80,1024]{1,0:T(8,128)(2,1)S(1)} %convert_element_type.86, bf16[1024,3,1024]{2,0,1:T(8,128)(2,1)} %param.10), kind=kOutput, calls=%fused_computation.72 | convolution fusion | flops 167854080 | bytes 2424832 | tf_op jit(solution)/shard_map/dot_general | solution.py:64
  107.6 2.1 %fusion.56 = bf16[80,1024]{1,0:T(8,128)(2,1)S(1)} fusion(bf16[80,1024]{1,0:T(8,128)(2,1)S(1)} %convert_element_type.86, bf16[1024,3,1024]{2,0,1:T(8,128)(2,1)} %param.10), kind=kOutput, calls=%fused_computation.73 | convolution fusion | flops 167854080 | bytes 2424832 | tf_op jit(solution)/shard_map/dot_general | solution.py:64
  109.7 0.2 reshape.176
  109.9 0.2 reshape.177
  110.1 1.2 convolution_multiply_fusion
  111.3 0.4 fusion.130
  111.7 2.1 %fusion.50 = bf16[80,1024]{1,0:T(8,128)(2,1)S(1)} fusion(bf16[80,1024]{1,0:T(8,128)(2,1)S(1)} %convert_element_type.86, bf16[1024,3,1024]{2,0,1:T(8,128)(2,1)} %param.10), kind=kOutput, calls=%fused_computation.71 | convolution fusion | flops 167854080 | bytes 2424832 | tf_op jit(solution)/shard_map/dot_general | solution.py:64
  113.8 0.2 reshape.175
  114.0 1.7 %fusion.48 = bf16[2,40,16,64]{3,1,2,0:T(8,128)(2,1)S(1)} fusion(bf16[2,40,16,64]{3,2,1,0:T(8,128)(2,1)S(1)} %reshape.175, f32[2,16,40]{2,1,0:T(8,128)S(1)} %fusion.130, f32[2,16,40,40]{2,3,1,0:T(8,128)} %convolution_multiply_fusion), kind=kOutput, calls=%fused_computation.67 | convolution fusion | flops 6790439 | bytes 537600 | tf_op jit(solution)/shard_map/rhqk,rkhd->rqhd/dot_general | solution.py:76
  115.8 0.2 reshape.178
  116.1 1.2 fusion.49
  (28 shorter events, 0.4 us)
Async XLA Ops:
  6.5 109.6 %copy-start = (bf16[1024,1024]{1,0:T(8,128)(2,1)S(1)}, bf16[1024,1024]{1,0:T(8,128)(2,1)}, u32[]{:S(2)}) copy-start(bf16[1024,1024]{1,0:T(8,128)(2,1)} %param.11) | copy-start | bytes 6291460
  6.5 14.3 %copy-start.6 = (bf16[3,3,69,256]{3,2,1,0:T(8,128)(2,1)S(1)}, bf16[3,3,69,256]{3,2,1,0:T(8,128)(2,1)}, u32[]{:S(2)}) copy-start(bf16[3,3,69,256]{3,2,1,0:T(8,128)(2,1)} %param.7) | copy-start | bytes 953860
  6.5 81.3 %all-gather.2.cloned.1.call-start = ((), (), s32[]{:S(2)}) async-start(), calls=%async_computation.1 | async-start | bytes 8912896 | tf_op jit(solution)/shard_map/all_gather | solution.py:97
  8.0 3.7 %collective-permute-start = (bf16[1,40,69]{2,1,0:T(8,128)(2,1)S(1)}, bf16[1,40,69]{2,1,0:T(8,128)(2,1)S(1)}, u32[]{:S(2)}, u32[]{:S(2)}) collective-permute-start(bf16[1,40,69]{2,1,0:T(8,128)(2,1)S(1)} %get-tuple-element.34), channel_id=1, source_target_pairs={{0,4},{4,8},{8,12},{1,5},{5,9},{9,13},{2,6},{6,10},{10,14},{3,7},{... | collective-permute-start | bytes 16568 | tf_op jit(solution)/shard_map/ppermute | solution.py:22
  10.3 5.2 %collective-permute-start.1 = (bf16[1,40,69]{2,1,0:T(8,128)(2,1)S(1)}, bf16[1,40,69]{2,1,0:T(8,128)(2,1)S(1)}, u32[]{:S(2)}, u32[]{:S(2)}) collective-permute-start(bf16[1,40,69]{2,1,0:T(8,128)(2,1)S(1)} %get-tuple-element.33), channel_id=1, source_target_pairs={{4,0},{8,4},{12,8},{5,1},{9,5},{13,9},{6,2},{10,6},{14,10},{7,3},{... | collective-permute-start | bytes 16568 | tf_op jit(solution)/shard_map/ppermute | solution.py:24
  17.0 5.6 %collective-permute-start.2 = (bf16[34,1,69]{2,1,0:T(2,128)(2,1)S(1)}, bf16[34,1,69]{2,1,0:T(2,128)(2,1)S(1)}, u32[]{:S(2)}, u32[]{:S(2)}) collective-permute-start(bf16[34,1,69]{2,1,0:T(2,128)(2,1)S(1)} %get-tuple-element.28), channel_id=1, source_target_pairs={{0,1},{1,2},{2,3},{3,0},{4,5},{5,6},{6,7},{7,4},{8,9},{9,10},{10,1... | collective-permute-start | bytes 14084 | tf_op jit(solution)/shard_map/ppermute | solution.py:22
  18.6 4.0 %collective-permute-start.3 = (bf16[34,1,69]{2,1,0:T(2,128)(2,1)S(1)}, bf16[34,1,69]{2,1,0:T(2,128)(2,1)S(1)}, u32[]{:S(2)}, u32[]{:S(2)}) collective-permute-start(bf16[34,1,69]{2,1,0:T(2,128)(2,1)S(1)} %get-tuple-element.29), channel_id=1, source_target_pairs={{1,0},{2,1},{3,2},{0,3},{5,4},{6,5},{7,6},{4,7},{9,8},{10,9},{11,1... | collective-permute-start | bytes 14084 | tf_op jit(solution)/shard_map/ppermute | solution.py:24
  24.0 1.0 copy-start.4
  27.2 0.8 copy-start.1
  28.0 6.2 %collective-permute-start.4 = (bf16[1,40,256]{2,1,0:T(8,128)(2,1)S(1)}, bf16[1,40,256]{2,1,0:T(8,128)(2,1)S(1)}, u32[]{:S(2)}, u32[]{:S(2)}) collective-permute-start(bf16[1,40,256]{2,1,0:T(8,128)(2,1)S(1)} %get-tuple-element.17), channel_id=1, source_target_pairs={{0,4},{4,8},{8,12},{1,5},{5,9},{9,13},{2,6},{6,10},{10,14},{3,7},{... | collective-permute-start | bytes 61448 | tf_op jit(solution)/shard_map/ppermute | solution.py:22
  31.4 3.6 %collective-permute-start.5 = (bf16[1,40,256]{2,1,0:T(8,128)(2,1)S(1)}, bf16[1,40,256]{2,1,0:T(8,128)(2,1)S(1)}, u32[]{:S(2)}, u32[]{:S(2)}) collective-permute-start(bf16[1,40,256]{2,1,0:T(8,128)(2,1)S(1)} %get-tuple-element.18), channel_id=1, source_target_pairs={{4,0},{8,4},{12,8},{5,1},{9,5},{13,9},{6,2},{10,6},{14,10},{7,3},{... | collective-permute-start | bytes 61448 | tf_op jit(solution)/shard_map/ppermute | solution.py:24
  34.2 7.5 %copy-start.5 = (bf16[3,3,256,256]{3,2,1,0:T(8,128)(2,1)S(1)}, bf16[3,3,256,256]{3,2,1,0:T(8,128)(2,1)}, u32[]{:S(2)}) copy-start(bf16[3,3,256,256]{3,2,1,0:T(8,128)(2,1)} %param.8) | copy-start | bytes 3538948
  36.0 6.7 %collective-permute-start.6 = (bf16[34,1,256]{2,1,0:T(2,128)(2,1)S(1)}, bf16[34,1,256]{2,1,0:T(2,128)(2,1)S(1)}, u32[]{:S(2)}, u32[]{:S(2)}) collective-permute-start(bf16[34,1,256]{2,1,0:T(2,128)(2,1)S(1)} %get-tuple-element.13), channel_id=1, source_target_pairs={{0,1},{1,2},{2,3},{3,0},{4,5},{5,6},{6,7},{7,4},{8,9},{9,10},{10,1... | collective-permute-start | bytes 52232 | tf_op jit(solution)/shard_map/ppermute | solution.py:22
  37.4 5.3 %collective-permute-start.7 = (bf16[34,1,256]{2,1,0:T(2,128)(2,1)S(1)}, bf16[34,1,256]{2,1,0:T(2,128)(2,1)S(1)}, u32[]{:S(2)}, u32[]{:S(2)}) collective-permute-start(bf16[34,1,256]{2,1,0:T(2,128)(2,1)S(1)} %get-tuple-element.14), channel_id=1, source_target_pairs={{1,0},{2,1},{3,2},{0,3},{5,4},{6,5},{7,6},{4,7},{9,8},{10,9},{11,1... | collective-permute-start | bytes 52232 | tf_op jit(solution)/shard_map/ppermute | solution.py:24
  41.7 1.1 copy-start.2
  47.7 2.7 %copy-start.3 = (f32[8,4,10,4,256]{4,3,2,1,0:T(4,128)S(1)}, f32[8,4,10,4,256]{4,3,2,1,0:T(4,128)}, u32[]{:S(2)}) copy-start(f32[8,4,10,4,256]{4,3,2,1,0:T(4,128)} %reshape.162) | copy-start | bytes 3932164
Sparse Core Ops, SparseCore 0:
  9.6 78.2 all-gather.1
where the time goes:
time: 125 us; the launch traced here: 124 us
  waiting for transfers between devices  40.6 us (32%)
  matrix products  23.6 us (19%)
  starting transfers between devices  16.4 us (13%)
  between operations  13.7 us (11%)
  blocking collectives  12 us (10%)
  other arithmetic  9.05 us (7%)
  local copies, waits for them, and re-layouts  8.86 us (7%)
    all_gather x1, waiting for transfers between devices, on_device(): lax.all_gather(down_weight, ('lat', 'lon'), axis=0, tiled=True)  33.4 us
    all_to_all x1, blocking collectives, on_device(): lax.all_to_all(tokens, 'lon', split_axis=0, concat_axis=1, tiled=True)  12 us
    ppermute x4, starting transfers between devices, extended(): lax.ppermute(tail, axis, [(i, (i + 1) % count) for i in range(ends)])  8.72 us
    dot_general x18, matrix products, convolve_tile(): jnp.dot(window, kernel[row_shift, col_shift], preferred_element_type=jnp....  7.94 us
    ppermute x4, starting transfers between devices, extended(): lax.ppermute(head, axis, [((i + 1) % count, i) for i in range(ends)])  7.7 us
    dot_general x3, matrix products, project(): jnp.dot(normed, weight, preferred_element_type=jnp.float32)  6.24 us
    dot_general x1, matrix products, on_device(): jnp.dot(patches, lax.all_gather(down_weight, ('lat', 'lon'), axis=0, tile...  4.94 us
    ppermute x4, waiting for transfers between devices, extended(): lax.ppermute(head, axis, [((i + 1) % count, i) for i in range(ends)])  4.66 us
  transfers between devices with their start and end apart: 9, of which 5 were waited for; matrix products, arithmetic and copies ran while one was open for 18% of the time, Pallas kernels for 0%

commit v1 on v0

--- a/solution.py
+++ b/solution.py
@@ -80,23 +80,45 @@
 
 
 def on_device(fields, first_kernel, second_kernel, down_weight, projections, output_weight):
+    groups, lats = lax.axis_size("groups"), lax.axis_size("lat")
+    part = D // groups
+    half = lax.dynamic_slice_in_dim(down_weight, lax.axis_index("groups") * part, part, axis=1)
+    weights = lax.all_gather(half, ("groups", "lon"), axis=0, tiled=True)
     row_count, col_count = (fields.shape[0], fields.shape[1])
     first = jax.nn.gelu(
-        convolve_tile(extend(fields, 1), first_kernel, row_count, col_count)
+        convolve_tile(extend(fields, 2), first_kernel, row_count + 2, col_count + 2)
     ).astype(jnp.bfloat16)
-    middle = convolve_tile(extend(first, 1), second_kernel, row_count, col_count)
-    second = (first.astype(jnp.float32) + jax.nn.gelu(middle)).astype(jnp.bfloat16)
+    lat = lax.axis_index("lat")
+    row = lax.broadcasted_iota(jnp.int32, first.shape, 0)
+    outside = ((row == 0) & (lat == 0)) | ((row == row_count + 1) & (lat == lats - 1))
+    first = jnp.where(outside, jnp.zeros_like(first), first)
+    middle = convolve_tile(first, second_kernel, row_count, col_count)
+    own = first[1:-1, 1:-1]
+    second = (own.astype(jnp.float32) + jax.nn.gelu(middle)).astype(jnp.bfloat16)
     token_rows, token_cols = (row_count // 4, col_count // 4)
+    count = token_rows * token_cols
+    depth = 16 * C // lats
     patches = (
         second.reshape(token_rows, 4, token_cols, 4, C)
-        .transpose(0, 2, 1, 3, 4)
-        .reshape(token_rows * token_cols, 16 * C)
+        .transpose(1, 3, 0, 2, 4)
+        .reshape(lats, 16 // lats, count, C)
     )
-    tokens = jnp.dot(
-        patches,
-        lax.all_gather(down_weight, ("lat", "lon"), axis=0, tiled=True),
-        preferred_element_type=jnp.float32,
+    patches = lax.all_to_all(patches, "lat", split_axis=0, concat_axis=0, tiled=True)
+    patches = patches.transpose(0, 2, 1, 3).reshape(lats * count, depth)
+    sums = jnp.concatenate(
+        [
+            jnp.dot(
+                patches,
+                weights[g * depth : (g + 1) * depth],
+                preferred_element_type=jnp.float32,
+            )
+            for g in range(groups)
+        ],
+        axis=1,
     )
+    sums = sums.astype(jnp.bfloat16).reshape(lats, count, D)
+    sums = lax.all_to_all(sums, "lat", split_axis=0, concat_axis=0, tiled=True)
+    tokens = jnp.sum(sums.astype(jnp.float32), axis=0)
     tokens = tokens.astype(jnp.bfloat16).reshape(token_rows, token_cols, D)
     band = lax.all_to_all(tokens, "lon", split_axis=0, concat_axis=1, tiled=True)
     mixed = attention(band, projections[:, 0], projections[:, 1], projections[:, 2])

time: 125 us -> 120 us (0.960)
  waiting for transfers between devices: 40.6 us -> 2.92 us
  blocking collectives: 12 us -> 41.2 us
  local copies, waits for them, and re-layouts: 8.86 us -> 22.7 us
  starting transfers between devices: 16.4 us -> 7.52 us
  other arithmetic: 9.05 us -> 5.43 us
  matrix products: 23.6 us -> 25.6 us
    all_gather x1, waiting for transfers between devices: 33.4 us -> 0.02 us  [on_device(): weights = lax.all_gather(half, ('groups', 'lon'), axis=0, tiled=True)]
    all_to_all x0 -> x2, blocking collectives: none -> 28 us  [the longest x1 15.3 us: on_device(): lax.all_to_all(patches, 'lat', split_axis=0, concat_axis=0, tiled=True)]
    reshape x1 -> x10, local copies, waits for them, and re-layouts: 0.48 us -> 9.69 us  [the longest x9 9.54 us: convolve_tile(): window = padded[row_shift:row_shift + row_count, col_shift:col_shift + co...]
    ppermute x4 -> x2, starting transfers between devices: 8.72 us -> 3.97 us  [extended(): lax.ppermute(tail, axis, [(i, (i + 1) % count) for i in range(ends)])]
    dot_general x18, matrix products: 7.94 us -> 12.5 us  [convolve_tile(): jnp.dot(window, kernel[row_shift, col_shift], preferred_element_type=jnp....]
    ppermute x4 -> x2, starting transfers between devices: 7.7 us -> 3.54 us  [extended(): lax.ppermute(head, axis, [((i + 1) % count, i) for i in range(ends)])]
    ppermute x4 -> x2, waiting for transfers between devices: 4.66 us -> 1.16 us  [extended(): lax.ppermute(head, axis, [((i + 1) % count, i) for i in range(ends)])]
    unnamed x15 -> x30, local copies, waits for them, and re-layouts: 1.54 us -> 4.8 us
  transfers between devices with their start and end apart: 9 -> 5, of which waited for: 5 -> 2; matrix products, arithmetic and copies ran while one was open for 18% -> 28% of each run, Pallas kernels for 0% -> 0%
where the time goes in v1:
time: 120 us; the launch traced here: 119 us
  blocking collectives  41.2 us (34%)
  matrix products  25.6 us (21%)
  local copies, waits for them, and re-layouts  22.7 us (19%)
  between operations  13.8 us (12%)
  starting transfers between devices  7.52 us (6%)
  other arithmetic  5.43 us (5%)
  waiting for transfers between devices  2.92 us (2%)
    all_to_all x1, blocking collectives, on_device(): lax.all_to_all(patches, 'lat', split_axis=0, concat_axis=0, tiled=True)  15.3 us
    all_to_all x1, blocking collectives, on_device(): lax.all_to_all(tokens, 'lon', split_axis=0, concat_axis=1, tiled=True)  13.2 us
    all_to_all x1, blocking collectives, on_device(): sums = lax.all_to_all(sums, 'lat', split_axis=0, concat_axis=0, tiled=True)  12.7 us
    dot_general x18, matrix products, convolve_tile(): jnp.dot(window, kernel[row_shift, col_shift], preferred_element_type=jnp....  12.5 us
    reshape x9, local copies, waits for them, and re-layouts, convolve_tile(): window = padded[row_shift:row_shift + row_count, col_shift:col_shift + co...  9.54 us
    dot_general x3, matrix products, project(): jnp.dot(normed, weight, preferred_element_type=jnp.float32)  6.25 us
    unnamed x30, local copies, waits for them, and re-layouts  4.8 us
    ppermute x2, starting transfers between devices, extended(): lax.ppermute(tail, axis, [(i, (i + 1) % count) for i in range(ends)])  3.97 us
  transfers between devices with their start and end apart: 5, of which 2 were waited for; matrix products, arithmetic and copies ran while one was open for 28% of the time, Pallas kernels for 0%

profile of v1, /device:TPU:0, one launch (start us, length us, event | category | flops | bytes accessed | tf_op | source)
XLA Modules:
  0.0 119.2 jit_solution(15671510361582318667)
XLA Ops:
  6.5 0.9 fusion.98
  7.4 2.3 %collective-permute-start = (bf16[2,40,69]{2,1,0:T(8,128)(2,1)S(1)}, bf16[2,40,69]{2,1,0:T(8,128)(2,1)S(1)}, u32[]{:S(2)}, u32[]{:S(2)}) collective-permute-start(bf16[2,40,69]{2,1,0:T(8,128)(2,1)S(1)} %get-tuple-element.29), channel_id=1, source_target_pairs={{0,4},{4,8},{8,12},{1,5},{5,9},{9,13},{2,6},{6,10},{10,14},{3,7},{... | collective-permute-start | bytes 33128 | tf_op jit(solution)/shard_map/ppermute | solution.py:22
  9.8 1.3 %collective-permute-start.1 = (bf16[2,40,69]{2,1,0:T(8,128)(2,1)S(1)}, bf16[2,40,69]{2,1,0:T(8,128)(2,1)S(1)}, u32[]{:S(2)}, u32[]{:S(2)}) collective-permute-start(bf16[2,40,69]{2,1,0:T(8,128)(2,1)S(1)} %get-tuple-element.28), channel_id=1, source_target_pairs={{4,0},{8,4},{12,8},{5,1},{9,5},{13,9},{6,2},{10,6},{14,10},{7,3},{... | collective-permute-start | bytes 33128 | tf_op jit(solution)/shard_map/ppermute | solution.py:24
  11.1 1.7 %constant_dynamic-slice_fusion = bf16[256,512]{1,0:T(8,128)(2,1)} fusion(bf16[256,1024]{1,0:T(8,128)(2,1)} %param.9, s32[]{:T(128)S(6)} %select_n.8), kind=kLoop, calls=%fused_computation.130 | loop fusion | bytes 524292 | tf_op jit(solution)/shard_map/dynamic_slice | solution.py:85
  12.8 1.0 constant_dynamic-update-slice_fusion.1
  13.9 1.2 collective-permute-done.1
  15.1 1.6 %collective-permute-start.2 = (bf16[36,2,69]{2,1,0:T(2,128)(2,1)S(1)}, bf16[36,2,69]{2,1,0:T(2,128)(2,1)S(1)}, u32[]{:S(2)}, u32[]{:S(2)}) collective-permute-start(bf16[36,2,69]{2,1,0:T(2,128)(2,1)S(1)} %get-tuple-element.26), channel_id=1, source_target_pairs={{0,1},{1,2},{2,3},{3,0},{4,5},{5,6},{6,7},{7,4},{8,9},{9,10},{10,1... | collective-permute-start | bytes 29816 | tf_op jit(solution)/shard_map/ppermute | solution.py:22
  16.7 2.2 %collective-permute-start.3 = (bf16[36,2,69]{2,1,0:T(2,128)(2,1)S(1)}, bf16[36,2,69]{2,1,0:T(2,128)(2,1)S(1)}, u32[]{:S(2)}, u32[]{:S(2)}) collective-permute-start(bf16[36,2,69]{2,1,0:T(2,128)(2,1)S(1)} %get-tuple-element.27), channel_id=1, source_target_pairs={{1,0},{2,1},{3,2},{0,3},{5,4},{6,5},{7,6},{4,7},{9,8},{10,9},{11,1... | collective-permute-start | bytes 29816 | tf_op jit(solution)/shard_map/ppermute | solution.py:24
  18.9 1.7 %collective-permute-done.2 = bf16[36,2,69]{2,1,0:T(2,128)(2,1)S(1)} collective-permute-done((bf16[36,2,69]{2,1,0:T(2,128)(2,1)S(1)}, bf16[36,2,69]{2,1,0:T(2,128)(2,1)S(1)}, u32[]{:S(2)}, u32[]{:S(2)}) %collective-permute-start.2) | collective-permute-done | bytes 9968 | tf_op jit(solution)/shard_map/ppermute | solution.py:22
  20.7 1.5 %pad_maximum_fusion.2 = (bf16[34,42,69]{2,1,0:T(8,128)(2,1)}, bf16[34,42,69]{2,1,0:T(8,128)(2,1)}, bf16[34,42,69]{2,1,0:T(8,128)(2,1)}, bf16[34,42,69]{2,1,0:T(8...) fusion(bf16[36,2,69]{2,1,0:T(2,128)(2,1)S(1)} %collective-permute-done.3, ...), kind=kLoop, calls=%fused_computation.75 | loop fusion | flops 2364768 | bytes 1400976 | tf_op jit(solution)/shard_map/concatenate | solution.py:20
  22.2 0.9 reshape.161
  23.5 0.9 reshape.162
  24.3 1.9 %reshape.163 = bf16[1428,69]{1,0:T(8,128)(2,1)} reshape(bf16[34,42,69]{2,1,0:T(8,128)(2,1)} %get-tuple-element.18) | data formatting | bytes 394128 | tf_op jit(solution)/shard_map/reshape | solution.py:42
  26.2 1.9 %reshape.164 = bf16[1428,69]{1,0:T(8,128)(2,1)} reshape(bf16[34,42,69]{2,1,0:T(8,128)(2,1)} %get-tuple-element.23) | data formatting | bytes 394128 | tf_op jit(solution)/shard_map/reshape | solution.py:42
  28.2 0.9 reshape.165
  29.0 2.0 %reshape.166 = bf16[1428,69]{1,0:T(8,128)(2,1)} reshape(bf16[34,42,69]{2,1,0:T(8,128)(2,1)} %get-tuple-element.19) | data formatting | bytes 394128 | tf_op jit(solution)/shard_map/reshape | solution.py:42
  31.0 0.9 reshape.167
  32.0 2.2 %fusion.77 = f32[1428,256]{1,0:T(8,128)} fusion(bf16[1428,69]{1,0:T(8,128)(2,1)S(1)} %copy-done.10, bf16[3,3,69,256]{3,2,1,0:T(8,128)(2,1)} %param.7), kind=kOutput, calls=%fused_computation.111 | convolution fusion | flops 50448384 | bytes 1696200 | tf_op jit(solution)/shard_map/dot_general | solution.py:43
  34.2 2.3 %fusion.70 = f32[1428,256]{1,0:T(8,128)} fusion(bf16[1428,69]{1,0:T(8,128)(2,1)S(1)} %reshape.168, bf16[3,3,69,256]{3,2,1,0:T(8,128)(2,1)} %param.7), kind=kOutput, calls=%fused_computation.104 | convolution fusion | flops 50448384 | bytes 1696200 | tf_op jit(solution)/shard_map/dot_general | solution.py:43
  36.7 1.8 %convolution_add_fusion.14 = f32[1428,256]{1,0:T(8,128)S(1)} fusion(f32[1428,256]{1,0:T(8,128)} %fusion.77, bf16[1428,69]{1,0:T(8,128)(2,1)S(1)} %copy-done.4, bf16[3,3,69,256]{3,2,1,0:T(8,128)(2,1)} %param.7), kind=kOutput, calls=%fused_computation.15 | convolution fusion | flops 50813952 | bytes 3162568 | tf_op jit(solution)/shard_map/dot_general | solution.py:43
  38.6 0.3 convolution_add_fusion.13
  38.9 0.6 copy-done.8
  39.6 0.3 convolution_add_fusion.12
  39.9 0.6 copy-done.7
  40.5 0.3 convolution_add_fusion.11
  40.9 0.6 copy-done.6
  41.5 0.3 convolution_add_fusion.10
  41.9 1.0 copy-done.1
  43.0 0.4 fusion.1
  43.3 1.5 %convolution_add_fusion.8 = f32[1428,256]{1,0:T(8,128)} fusion(f32[1428,256]{1,0:T(8,128)S(1)} %fusion.1, bf16[1428,69]{1,0:T(8,128)(2,1)S(1)} %reshape.169, bf16[3,3,69,256]{3,2,1,0:T(8,128)(2,1)S(1)} %copy-done.12), kind=kOutput, calls=%fused_computation.9 | convolution fusion | flops 50813952 | bytes 3332096 | tf_op jit(solution)/shard_map/dot_general | solution.py:43
  44.8 2.5 %reshape.170 = f32[34,42,256]{2,1,0:T(8,128)} reshape(f32[1428,256]{1,0:T(8,128)} %convolution_add_fusion.8) | data formatting | bytes 2924544 | tf_op jit(solution)/shard_map/reshape | solution.py:46
  47.3 2.1 %fusion.41 = bf16[34,42,256]{2,1,0:T(8,128)(2,1)S(1)} fusion(f32[34,42,256]{2,1,0:T(8,128)} %reshape.170, pred[34]{0:T(512)(128)(4,1)S(1)} %and_or_fusion), kind=kLoop, calls=%fused_computation.59 | loop fusion | flops 3655680 | bytes 2193442 | tf_op jit(solution)/shard_map/jit(_where)/select_n | solution.py:94
  49.4 0.6 fusion.95
  50.0 0.7 copy-done.11
  50.7 0.3 fusion.58
  51.0 0.3 convolution_add_fusion.7
  51.3 0.3 convolution_add_fusion.6
  51.7 0.3 convolution_add_fusion.5
  52.0 0.3 convolution_add_fusion.4
  52.4 0.3 convolution_add_fusion.3
  52.7 0.3 convolution_add_fusion.2
  53.0 0.3 convolution_add_fusion.1
  53.4 0.3 convolution_add_fusion
  53.7 0.6 fusion.28
  54.5 0.2 copy.30
  54.7 15.3 %all_to_all.19 = bf16[4,4,80,256]{3,1,2,0:T(4,128)(2,1)S(1)} all-to-all(bf16[4,4,80,256]{3,1,2,0:T(4,128)(2,1)S(1)} %bitcast.137), channel_id=1, replica_groups=mesh['groups'=2,'lat'=4,'lon'=4] {'lat'}, dimensions={0} | all-to-all | bytes 1310720 | tf_op jit(solution)/shard_map/all_to_all | solution.py:106
  70.0 0.5 dot_general.98
  70.6 1.9 %convolution_convert_fusion.1 = bf16[4,80,512]{2,1,0:T(8,128)(2,1)S(1)} fusion(bf16[4,80,1024]{2,1,0:T(8,128)(2,1)S(1)} %dot_general.98, bf16[2048,512]{1,0:T(8,128)(2,1)} %all-gather.2.cloned.1.call-done), kind=kOutput, calls=%fused_computation.49 | convolution fusion | flops 335708160 | bytes 2031616 | tf_op jit(solution)/shard_map/dot_general | solution.py:110
  72.5 0.5 convolution_convert_fusion
  73.0 12.7 %all_to_all.20 = bf16[4,80,1024]{2,1,0:T(8,128)(2,1)S(1)} all-to-all(bf16[4,80,1024]{2,1,0:T(8,128)(2,1)S(1)} %pad_maximum_fusion), channel_id=1, replica_groups=mesh['groups'=2,'lat'=4,'lon'=4] {'lat'}, dimensions={0} | all-to-all | bytes 1310720 | tf_op jit(solution)/shard_map/all_to_all | solution.py:120
  85.9 13.2 %all_to_all.21 = bf16[8,10,1024]{2,1,0:T(8,128)(2,1)S(1)} all-to-all(bf16[8,10,1024]{2,1,0:T(8,128)(2,1)S(1)} %reshape.183), channel_id=1, replica_groups=mesh['groups'=2,'lat'=4,'lon'=4] {'lon'}, dimensions={0} | all-to-all | bytes 327680 | tf_op jit(solution)/shard_map/all_to_all | solution.py:123
  99.5 0.3 multiply_reduce_fusion
  99.9 0.2 multiply_convert_fusion
  100.3 2.1 %fusion.35 = bf16[80,1024]{1,0:T(8,128)(2,1)S(1)} fusion(bf16[80,1024]{1,0:T(8,128)(2,1)S(1)} %convert_element_type.76, bf16[1024,3,1024]{2,0,1:T(8,128)(2,1)} %param.10), kind=kOutput, calls=%fused_computation.55 | convolution fusion | flops 167854080 | bytes 2424832 | tf_op jit(solution)/shard_map/dot_general | solution.py:64
  102.4 2.1 %fusion.38 = bf16[80,1024]{1,0:T(8,128)(2,1)S(1)} fusion(bf16[80,1024]{1,0:T(8,128)(2,1)S(1)} %convert_element_type.76, bf16[1024,3,1024]{2,0,1:T(8,128)(2,1)} %param.10), kind=kOutput, calls=%fused_computation.56 | convolution fusion | flops 167854080 | bytes 2424832 | tf_op jit(solution)/shard_map/dot_general | solution.py:64
  104.5 0.2 reshape.185
  104.7 0.2 reshape.186
  104.9 1.2 convolution_multiply_fusion
  106.1 0.4 fusion.99
  106.5 2.1 %fusion.32 = bf16[80,1024]{1,0:T(8,128)(2,1)S(1)} fusion(bf16[80,1024]{1,0:T(8,128)(2,1)S(1)} %convert_element_type.76, bf16[1024,3,1024]{2,0,1:T(8,128)(2,1)} %param.10), kind=kOutput, calls=%fused_computation.54 | convolution fusion | flops 167854080 | bytes 2424832 | tf_op jit(solution)/shard_map/dot_general | solution.py:64
  108.6 0.2 reshape.184
  108.8 1.8 %fusion.30 = bf16[2,40,16,64]{3,1,2,0:T(8,128)(2,1)S(1)} fusion(bf16[2,40,16,64]{3,2,1,0:T(8,128)(2,1)S(1)} %reshape.184, f32[2,16,40]{2,1,0:T(8,128)S(1)} %fusion.99, f32[2,16,40,40]{2,3,1,0:T(8,128)} %convolution_multiply_fusion), kind=kOutput, calls=%fused_computation.51 | convolution fusion | flops 6790439 | bytes 537600 | tf_op jit(solution)/shard_map/rhqk,rkhd->rqhd/dot_general | solution.py:76
  110.6 0.2 reshape.187
  111.2 1.2 fusion.31
  (50 shorter events, 2.2 us)
Async XLA Ops:
  6.5 104.6 %copy-start = (bf16[1024,1024]{1,0:T(8,128)(2,1)S(1)}, bf16[1024,1024]{1,0:T(8,128)(2,1)}, u32[]{:S(2)}) copy-start(bf16[1024,1024]{1,0:T(8,128)(2,1)} %param.11) | copy-start | bytes 6291460
  6.5 64.0 %all-gather.2.cloned.1.call-start = ((), (), s32[]{:S(2)}) async-start(), calls=%async_computation.3 | async-start | bytes 2359296 | tf_op jit(solution)/shard_map/all_gather | solution.py:86
  7.4 5.4 %collective-permute-start = (bf16[2,40,69]{2,1,0:T(8,128)(2,1)S(1)}, bf16[2,40,69]{2,1,0:T(8,128)(2,1)S(1)}, u32[]{:S(2)}, u32[]{:S(2)}) collective-permute-start(bf16[2,40,69]{2,1,0:T(8,128)(2,1)S(1)} %get-tuple-element.29), channel_id=1, source_target_pairs={{0,4},{4,8},{8,12},{1,5},{5,9},{9,13},{2,6},{6,10},{10,14},{3,7},{... | collective-permute-start | bytes 33128 | tf_op jit(solution)/shard_map/ppermute | solution.py:22
  9.8 5.2 %collective-permute-start.1 = (bf16[2,40,69]{2,1,0:T(8,128)(2,1)S(1)}, bf16[2,40,69]{2,1,0:T(8,128)(2,1)S(1)}, u32[]{:S(2)}, u32[]{:S(2)}) collective-permute-start(bf16[2,40,69]{2,1,0:T(8,128)(2,1)S(1)} %get-tuple-element.28), channel_id=1, source_target_pairs={{4,0},{8,4},{12,8},{5,1},{9,5},{13,9},{6,2},{10,6},{14,10},{7,3},{... | collective-permute-start | bytes 33128 | tf_op jit(solution)/shard_map/ppermute | solution.py:24
  15.1 5.6 %collective-permute-start.2 = (bf16[36,2,69]{2,1,0:T(2,128)(2,1)S(1)}, bf16[36,2,69]{2,1,0:T(2,128)(2,1)S(1)}, u32[]{:S(2)}, u32[]{:S(2)}) collective-permute-start(bf16[36,2,69]{2,1,0:T(2,128)(2,1)S(1)} %get-tuple-element.26), channel_id=1, source_target_pairs={{0,1},{1,2},{2,3},{3,0},{4,5},{5,6},{6,7},{7,4},{8,9},{9,10},{10,1... | collective-permute-start | bytes 29816 | tf_op jit(solution)/shard_map/ppermute | solution.py:22
  16.7 4.0 %collective-permute-start.3 = (bf16[36,2,69]{2,1,0:T(2,128)(2,1)S(1)}, bf16[36,2,69]{2,1,0:T(2,128)(2,1)S(1)}, u32[]{:S(2)}, u32[]{:S(2)}) collective-permute-start(bf16[36,2,69]{2,1,0:T(2,128)(2,1)S(1)} %get-tuple-element.27), channel_id=1, source_target_pairs={{1,0},{2,1},{3,2},{0,3},{5,4},{6,5},{7,6},{4,7},{9,8},{10,9},{11,1... | collective-permute-start | bytes 29816 | tf_op jit(solution)/shard_map/ppermute | solution.py:24
  26.2 4.7 %copy-start.3 = (bf16[34,42,69]{2,1,0:T(8,128)(2,1)S(1)}, bf16[34,42,69]{2,1,0:T(8,128)(2,1)}, u32[]{:S(2)}) copy-start(bf16[34,42,69]{2,1,0:T(8,128)(2,1)} %get-tuple-element.25) | copy-start | bytes 591196
  29.0 3.0 %copy-start.10 = (bf16[1428,69]{1,0:T(8,128)(2,1)S(1)}, bf16[1428,69]{1,0:T(8,128)(2,1)}, u32[]{:S(2)}) copy-start(bf16[1428,69]{1,0:T(8,128)(2,1)} %reshape.162) | copy-start | bytes 591196
  34.2 2.3 %copy-start.2 = (bf16[34,42,69]{2,1,0:T(8,128)(2,1)S(1)}, bf16[34,42,69]{2,1,0:T(8,128)(2,1)}, u32[]{:S(2)}) copy-start(bf16[34,42,69]{2,1,0:T(8,128)(2,1)} %get-tuple-element.17) | copy-start | bytes 591196
  34.2 2.5 %copy-start.4 = (bf16[1428,69]{1,0:T(8,128)(2,1)S(1)}, bf16[1428,69]{1,0:T(8,128)(2,1)}, u32[]{:S(2)}) copy-start(bf16[1428,69]{1,0:T(8,128)(2,1)} %reshape.161) | copy-start | bytes 591196
  36.7 1.8 %copy-start.9 = (bf16[1428,69]{1,0:T(8,128)(2,1)S(1)}, bf16[1428,69]{1,0:T(8,128)(2,1)}, u32[]{:S(2)}) copy-start(bf16[1428,69]{1,0:T(8,128)(2,1)} %reshape.163) | copy-start | bytes 591196
  36.7 1.8 %copy-start.12 = (bf16[3,3,69,256]{3,2,1,0:T(8,128)(2,1)S(1)}, bf16[3,3,69,256]{3,2,1,0:T(8,128)(2,1)}, u32[]{:S(2)}) copy-start(bf16[3,3,69,256]{3,2,1,0:T(8,128)(2,1)} %param.7) | copy-start | bytes 953860
  38.6 1.0 copy-start.8
  39.5 1.0 copy-start.7
  40.5 1.0 copy-start.6
  41.5 1.4 %copy-start.1 = (f32[1428,256]{1,0:T(8,128)S(1)}, f32[1428,256]{1,0:T(8,128)}, u32[]{:S(2)}) copy-start(f32[1428,256]{1,0:T(8,128)} %fusion.70) | copy-start | bytes 4386820
  41.5 1.4 %copy-start.5 = (bf16[1428,69]{1,0:T(8,128)(2,1)S(1)}, bf16[1428,69]{1,0:T(8,128)(2,1)}, u32[]{:S(2)}) copy-start(bf16[1428,69]{1,0:T(8,128)(2,1)} %reshape.167) | copy-start | bytes 591196
  49.4 1.3 %copy-start.11 = (bf16[3,3,256,256]{3,2,1,0:T(8,128)(2,1)S(1)}, bf16[3,3,256,256]{3,2,1,0:T(8,128)(2,1)}, u32[]{:S(2)}) copy-start(bf16[3,3,256,256]{3,2,1,0:T(8,128)(2,1)} %param.8) | copy-start | bytes 3538948
  70.5 1.9 %copy-start.13 = (bf16[2048,512]{1,0:T(8,128)(2,1)S(1)}, bf16[2048,512]{1,0:T(8,128)(2,1)}, u32[]{:S(2)}) copy-start(bf16[2048,512]{1,0:T(8,128)(2,1)} %all-gather.2.cloned.1.call-done) | copy-start | bytes 6291460
Sparse Core Ops, SparseCore 0:
  12.9 53.8 all-gather.1

commit v2 on v0

v2 whole, which is shorter than its diff:
```python
import functools

import jax
import jax.numpy as jnp
from jax import lax
from jax.experimental import pallas as pl
from jax.experimental.pallas import tpu as pltpu
from jax.sharding import PartitionSpec as P

C = 256
D = 1024
HD = 64
WIDE = 48
LANES = 128
MESH = pl.DeviceIdType.MESH


epsilon = 1e-05

SIDES = [(da, db) for da in (-1, 0, 1) for db in (-1, 0, 1) if (da, db) != (0, 0)]


def side_rows(da, db, rows, cols):
    return (2 if da else rows) * (8 if db else cols)


def encode_kernel(
    sizes,
    fields,
    k1_ref,
    k2_hbm,
    down,
    band,
    x3,
    xb,
    f_ref,
    s_ref,
    t_ref,
    pb,
    pr,
    qb,
    qr,
    tok,
    tokpad,
    tb,
    wbuf,
    k2,
    *rest,
):
    groups, lats, lons, rows, cols = sizes
    out_halo, in_halo = rest[:8], rest[8:16]
    (
        local_sem,
        halo_send,
        halo_recv,
        z_send,
        z_recv,
        x_send,
        x_recv,
        p_send,
        p_recv,
        q_send,
        q_recv,
        t_send,
        t_recv,
    ) = rest[16:]
    g, a, b = lax.axis_index("groups"), lax.axis_index("lat"), lax.axis_index("lon")
    part = D // groups
    count = (rows // 4) * (cols // 4)
    depth = 16 * C // lats
    shard = depth // lons
    cnt = count // lons
    cp = -(-cnt // 16) * 16

    k2_copy = pltpu.make_async_copy(k2_hbm, k2, local_sem.at[0])
    k2_copy.start()
    own_copies = [
        pltpu.make_async_copy(
            down.at[:, pl.ds(h * part, part)], wbuf.at[h, b], local_sem.at[1 + h]
        )
        for h in range(groups)
    ]
    for copy in own_copies:
        copy.start()

    barrier = pltpu.get_barrier_semaphore()

    def greet(i, _):
        gg = i // (lats * lons)
        aa = (i // lons) % lats
        bb = i % lons
        pl.semaphore_signal(barrier, inc=1, device_id=(gg, aa, bb), device_id_type=MESH)
        return 0

    lax.fori_loop(0, groups * lats * lons, greet, 0)

    x3[...] = jnp.zeros(x3.shape, jnp.float32)
    x3[4 : 4 + rows, 0:cols, 0 : fields.shape[2]] = fields[...].astype(jnp.float32)
    for n, (da, db) in enumerate(SIDES):
        r0, r1 = {-1: (4, 6), 0: (4, 4 + rows), 1: (2 + rows, 4 + rows)}[da]
        c0, c1 = {-1: (0, 8), 0: (0, cols), 1: (cols - 8, cols)}[db]
        out_halo[n][...] = x3[r0:r1, c0:c1, :].reshape(-1, LANES).astype(jnp.bfloat16)

    pl.semaphore_wait(barrier, groups * lats * lons)

    def halo(n):
        da, db = SIDES[n]
        return pltpu.make_async_remote_copy(
            src_ref=out_halo[n],
            dst_ref=in_halo[n],
            send_sem=halo_send.at[n],
            recv_sem=halo_recv.at[n],
            device_id=(g, jnp.clip(a + da, 0, lats - 1), lax.rem(b + db + lons, lons)),
            device_id_type=MESH,
        )

    def inside(index):
        return jnp.logical_and(index >= 0, index < lats)

    for n, (da, db) in enumerate(SIDES):
        if da == 0:
            halo(n).start()
        else:

            @pl.when(inside(a + da))
            def _():
                halo(n).start()

    def along(c, step):
        return pltpu.make_async_remote_copy(
            src_ref=wbuf.at[g, c],
            dst_ref=wbuf.at[g, c],
            send_sem=z_send.at[c, (step + 1) // 2],
            recv_sem=z_recv.at[c],
            device_id=(g, a, jnp.clip(b + step, 0, lons - 1)),
            device_id_type=MESH,
        )

    def across(c, j):
        gg = lax.rem(g + j, groups)
        return pltpu.make_async_remote_copy(
            src_ref=wbuf.at[g, c],
            dst_ref=wbuf.at[g, c],
            send_sem=x_send.at[c, j],
            recv_sem=x_recv.at[g, c],
            device_id=(gg, a, b),
            device_id_type=MESH,
        )

    def relay(s):
        for way in (1, -1):
            c = b - way * s

            @pl.when(jnp.logical_and(c >= 0, c < lons))
            def _():
                if s > 0:
                    along(c, way).wait_recv()

                @pl.when(jnp.logical_and(b + way >= 0, b + way < lons))
                def _():
                    along(c, way).start()

                if s > 0:
                    for j in range(1, groups):
                        across(c, j).start()

    for copy in own_copies:
        copy.wait()
    relay(0)

    lane = lax.broadcasted_iota(jnp.int32, (1, 8, LANES), 1)
    for n, (da, db) in enumerate(SIDES):

        def place(n=n, da=da, db=db):
            halo(n).wait_recv()
            r0, nr = {-1: (4 + rows, 2), 0: (4, rows), 1: (2, 2)}[da]
            value = in_halo[n][...].astype(jnp.float32)
            if db == 0:
                x3[r0 : r0 + nr, 0:cols, :] = value.reshape(nr, cols, LANES)
            else:
                value = value.reshape(nr, 8, LANES)
                if db < 0:
                    value = jnp.where(lane < 2, value, 0.0)
                else:
                    value = jnp.where(lane >= 6, value, 0.0)
                    r0 = r0 - 1
                x3[r0 : r0 + nr, cols : cols + 8, :] = x3[r0 : r0 + nr, cols : cols + 8, :] + value

        if da == 0:
            place()
        else:
            pl.when(inside(a - da))(place)
    xb[...] = x3[...].reshape(-1, LANES).astype(jnp.bfloat16)

    def conv(source, start, size, weights):
        total = [None] * 3
        for dr in range(3):
            window = source[pl.ds(pl.multiple_of(start + dr * WIDE, 16), size), :]
            for dc in range(3):
                term = jnp.dot(window, weights(dr, dc), preferred_element_type=jnp.float32)
                total[dc] = term if total[dc] is None else total[dc] + term
        whole = pltpu.roll(total[0], 1, 0) + total[1] + pltpu.roll(total[2], size - 1, 0)
        return whole[16 : size - 16]

    f_ref[0:16, :] = jnp.zeros((16, C), jnp.bfloat16)
    tail = (rows + 3) * WIDE
    f_ref[tail + 16 : tail + 32, :] = jnp.zeros((16, C), jnp.bfloat16)
    lo = jnp.where(a == 0, 2 * WIDE - 4, -1)
    hi = jnp.where(a == lats - 1, (rows + 2) * WIDE - 4, tail)

    def first_step(k, _):
        size = 5 * WIDE
        value = jax.nn.gelu(
            conv(xb, (5 * k + 1) * WIDE - 16, size + 32, lambda r, c: k1_ref[3 * r + c])
        )
        at = k * size + lax.broadcasted_iota(jnp.int32, (size, C), 0)
        value = jnp.where(jnp.logical_and(at >= lo, at < hi), value, 0.0)
        f_ref[pl.ds(pl.multiple_of(16 + k * size, 16), size), :] = value.astype(jnp.bfloat16)
        return 0

    lax.fori_loop(0, (rows + 3) // 5, first_step, 0)
    relay(1)
    k2_copy.wait()

    def second_step(k, _):
        size = 4 * WIDE
        value = jax.nn.gelu(
            conv(f_ref, (4 * k + 1) * WIDE, size + 32, lambda r, c: k2[r, c])
        )
        own = f_ref[pl.ds(pl.multiple_of(16 + (4 * k + 2) * WIDE, 16), size), :]
        value = own.astype(jnp.float32) + value
        for h in range(C // LANES):
            s_ref[h, pl.ds(pl.multiple_of(k * size, 16), size), :] = value[
                :, h * LANES : (h + 1) * LANES
            ]
        return 0

    halfway = rows // 8
    lax.fori_loop(0, halfway, second_step, 0)
    if lons > 2:
        relay(2)
    lax.fori_loop(halfway, rows // 4, second_step, 0)
    for s in range(3, lons):
        relay(s)

    wide = cols // 4
    for t in range(rows // 4):
        for p in range(4):
            for q in range(4):
                at = (4 * t + p) * WIDE + q
                for h in range(C // LANES):
                    to = (4 * p + q) * C + h * LANES
                    t_ref[t * wide : (t + 1) * wide, to : to + LANES] = s_ref[
                        h, pl.ds(at, wide, stride=4), :
                    ]
    for c in range(lats):
        pb[c * count : (c + 1) * count, :] = t_ref[:, c * depth : (c + 1) * depth].astype(
            jnp.bfloat16
        )

    def rows_of(ref, index, size):
        return ref.at[pl.ds(pl.multiple_of(index * size, 16), size)]

    def exchange(src, dst, size, send, recv, me, count_of, axis):
        def copy(j, incoming=False):
            other = lax.rem(me + j, count_of)
            target = (g, other, b) if axis == "lat" else (g, a, other)
            sender = lax.rem(me + count_of - j, count_of) if incoming else me
            return pltpu.make_async_remote_copy(
                src_ref=rows_of(src, other, size),
                dst_ref=rows_of(dst, sender, size),
                send_sem=send.at[j],
                recv_sem=recv.at[j],
                device_id=target,
                device_id_type=MESH,
            )

        for j in range(1, count_of):
            copy(j).start()
        mine = pl.ds(pl.multiple_of(me * size, 16), size)
        dst[mine, :] = src[mine, :]
        return copy

    to_k = exchange(pb, pr, count, p_send, p_recv, a, lats, "lat")

    def all_across(do):
        for s in range(1, lons):
            for way in (1, -1):
                c = b - way * s

                @pl.when(jnp.logical_and(c >= 0, c < lons))
                def _():
                    do(c)

    def take(c):
        for j in range(1, groups):
            gg = lax.rem(g + j, groups)
            pltpu.make_async_remote_copy(
                src_ref=wbuf.at[gg, c],
                dst_ref=wbuf.at[gg, c],
                send_sem=x_send.at[c, j],
                recv_sem=x_recv.at[gg, c],
                device_id=(gg, a, b),
                device_id_type=MESH,
            ).wait_recv()

    all_across(take)
    for j in range(1, lats):
        to_k(j, True).wait_recv()
    block = min(part, 256)
    for h in range(groups):
        for n in range(0, part, block):
            total = None
            for c in range(lons):
                term = jnp.dot(
                    pr[:, c * shard : (c + 1) * shard],
                    wbuf[h, c, :, n : n + block],
                    preferred_element_type=jnp.float32,
                )
                total = term if total is None else total + term
            qb[:, h * part + n : h * part + n + block] = total.astype(jnp.bfloat16)
    back = exchange(qb, qr, count, q_send, q_recv, a, lats, "lat")
    tokpad[...] = jnp.zeros(tokpad.shape, jnp.float32)
    for j in range(1, lats):
        back(j, True).wait_recv()
    total = qr[0:count, :].astype(jnp.float32)
    for c in range(1, lats):
        total = total + qr[c * count : (c + 1) * count, :].astype(jnp.float32)
    tok[...] = total
    for c in range(lons):
        tokpad[c * cp : c * cp + cnt, :] = tok[c * cnt : (c + 1) * cnt, :]
    tb[...] = tokpad[...].astype(jnp.bfloat16)
    to_rows = exchange(tb, band, cp, t_send, t_recv, b, lons, "lon")
    for j in range(1, lons):
        to_rows(j, True).wait_recv()

    for n, (da, db) in enumerate(SIDES):
        if da == 0:
            halo(n).wait_send()
        else:

            @pl.when(inside(a + da))
            def _():
                halo(n).wait_send()

    for s in range(lons):
        for way in (1, -1):
            c = b - way * s

            @pl.when(jnp.logical_and(c >= 0, c < lons))
            def _():
                @pl.when(jnp.logical_and(b + way >= 0, b + way < lons))
                def _():
                    along(c, way).wait_send()

                if s > 0:
                    for j in range(1, groups):
                        across(c, j).wait_send()

    for j in range(1, lats):
        to_k(j).wait_send()
        back(j).wait_send()
    for j in range(1, lons):
        to_rows(j).wait_send()


def encode(fields, first_kernel, second_kernel, down_weight):
    groups, lats, lons = (lax.axis_size(name) for name in ("groups", "lat", "lon"))
    rows, cols = fields.shape[0], fields.shape[1]
    count = (rows // 4) * (cols // 4)
    depth = 16 * C // lats
    cnt = count // lons
    cp = -(-cnt // 16) * 16
    padded = jnp.pad(
        first_kernel.reshape(9, -1, C), ((0, 0), (0, LANES - first_kernel.shape[2]), (0, 0))
    )
    halos = [
        pltpu.VMEM((side_rows(da, db, rows, cols), LANES), jnp.bfloat16) for da, db in SIDES
    ]
    dma = pltpu.SemaphoreType.DMA
    vmem = pl.BlockSpec(memory_space=pltpu.VMEM)
    anywhere = pl.BlockSpec(memory_space=pl.ANY)
    bf16, f32 = jnp.bfloat16, jnp.float32
    return pl.pallas_call(
        functools.partial(encode_kernel, (groups, lats, lons, rows, cols)),
        out_shape=jax.ShapeDtypeStruct((lons * cp, D), bf16),
        in_specs=[vmem, vmem, anywhere, anywhere],
        out_specs=vmem,
        scratch_shapes=[
            pltpu.VMEM((rows + 7, WIDE, LANES), f32),
            pltpu.VMEM(((rows + 7) * WIDE, LANES), bf16),
            pltpu.VMEM(((rows + 3) * WIDE + 32, C), bf16),
            pltpu.VMEM((C // LANES, rows * WIDE, LANES), f32),
            pltpu.VMEM((count, 16 * C), f32),
            pltpu.VMEM((lats * count, depth), bf16),
            pltpu.VMEM((lats * count, depth), bf16),
            pltpu.VMEM((lats * count, D), bf16),
            pltpu.VMEM((lats * count, D), bf16),
            pltpu.VMEM((count, D), f32),
            pltpu.VMEM((lons * cp, D), f32),
            pltpu.VMEM((lons * cp, D), bf16),
            pltpu.VMEM((groups, lons, depth // lons, D // groups), bf16),
            pltpu.VMEM(second_kernel.shape, bf16),
            *halos,
            *halos,
            dma((1 + groups,)),
            dma((8,)),
            dma((8,)),
            dma((lons, 2)),
            dma((lons,)),
            dma((lons, groups)),
            dma((groups, lons)),
            dma((lats,)),
            dma((lats,)),
            dma((lats,)),
            dma((lats,)),
            dma((lons,)),
            dma((lons,)),
        ],
        compiler_params=pltpu.CompilerParams(
            collective_id=0, has_side_effects=True, vmem_limit_bytes=44 * 1024 * 1024
        ),
    )(fields, padded, second_kernel, down_weight)


def attention(band, query_weight, key_weight, value_weight):
    row_count, token_count = (band.shape[0], band.shape[1])
    widened = band.astype(jnp.float32)
    average = jnp.mean(widened, axis=-1, keepdims=True)
    centred = widened - average
    spread = jnp.mean(centred * centred, axis=-1, keepdims=True)
    normed = (
        (centred * lax.rsqrt(spread + epsilon))
        .astype(jnp.bfloat16)
        .reshape(row_count * token_count, -1)
    )
    head_count = query_weight.shape[1] // HD

    def project(weight):
        return (
            jnp.dot(normed, weight, preferred_element_type=jnp.float32)
            .astype(jnp.bfloat16)
            .reshape(row_count, token_count, head_count, HD)
        )

    query = project(query_weight)
    keys = project(key_weight)
    values = project(value_weight)
    scores = jnp.einsum(
        "rqhd,rkhd->rhqk", query, keys, preferred_element_type=jnp.float32
    ) * HD ** (-0.5)
    probs = jax.nn.softmax(scores, axis=-1).astype(jnp.bfloat16)
    mixed = jnp.einsum("rhqk,rkhd->rqhd", probs, values, preferred_element_type=jnp.float32).astype(
        jnp.bfloat16
    )
    return mixed.reshape(row_count * token_count, head_count * HD)


def on_device(fields, first_kernel, second_kernel, down_weight, projections, output_weight):
    lons = lax.axis_size("lon")
    wide = fields.shape[1] // 4
    rows = fields.shape[0] // 4 // lons
    band = encode(fields, first_kernel, second_kernel, down_weight)
    band = band.reshape(lons, -1, D)[:, : rows * wide].reshape(lons, rows, wide, D)
    band = band.transpose(1, 0, 2, 3).reshape(rows, lons * wide, D)
    mixed = attention(band, projections[:, 0], projections[:, 1], projections[:, 2])
    summed = band.astype(jnp.float32).reshape(-1, D) + jnp.dot(
        mixed, output_weight, preferred_element_type=jnp.float32
    )
    return summed.astype(jnp.bfloat16).reshape(band.shape)


def solution(mesh):
    placed = (P(("groups", "lat"), "lon", None), P(), P(), P(("lat", "lon"), None), P(), P())
    return jax.shard_map(
        on_device,
        mesh=mesh,
        in_specs=placed,
        out_specs=P(("groups", "lat", "lon"), None, None),
        check_vma=False,
    )
```

time: 125 us -> 70 us (0.56)
  the two profiles are of different devices: /device:TPU:0 before, /device:TPU:1 now
where the time goes in v2:
time: 70 us; the launch traced here: 69.6 us
  Pallas kernels  52.3 us (75%)
  matrix products  10.7 us (15%)
  local copies, waits for them, and re-layouts  5.99 us (9%)
    pallas_call x1, Pallas kernels, encode(): pl.pallas_call(functools.partial(encode_kernel, (groups, lats, lons, rows...  52.3 us
    dot_general x3, matrix products, project(): jnp.dot(normed, weight, preferred_element_type=jnp.float32)  6.25 us
    unnamed x9, local copies, waits for them, and re-layouts  3.5 us
    dot_general x1, matrix products, attention(): jnp.einsum('rhqk,rkhd->rqhd', probs, values, preferred_element_type=jnp.f...  1.71 us

profile of v2, /device:TPU:1, one launch (start us, length us, event | category | flops | bytes accessed | tf_op | source)
XLA Modules:
  0.0 69.6 jit_solution(16238005335006772183)
XLA Ops:
  0.0 0.0 copy-start
  0.0 1.2 %pad.4.k1_ref = bf16[9,128,256]{2,1,0:T(8,128)(2,1)S(1)} pad(bf16[9,69,256]{2,1,0:T(8,128)(2,1)} %bitcast.41, bf16[]{:T(256)} %constant.6.clone.1), padding=0_0x0_59x0_0 | pad | bytes 907778 | tf_op jit(solution)/shard_map/jit(_pad)/pad | solution.py:374
  1.2 0.0 copy-start.1
  1.2 1.3 %copy-done.1 = bf16[3,3,256,256]{3,2,1,0:T(8,128)(2,1)S(1)} copy-done((bf16[3,3,256,256]{3,2,1,0:T(8,128)(2,1)S(1)}, bf16[3,3,256,256]{3,2,1,0:T(8,128)(2,1)}, u32[]{:S(2)}) %copy-start.1) | copy-done | bytes 1179672
  2.5 0.0 copy-start.2
  2.5 1.0 %copy-done.2 = bf16[256,1024]{1,0:T(8,128)(2,1)S(1)} copy-done((bf16[256,1024]{1,0:T(8,128)(2,1)S(1)}, bf16[256,1024]{1,0:T(8,128)(2,1)}, u32[]{:S(2)}) %copy-start.2) | copy-done | bytes 524312
  3.5 0.0 copy-start.3
  3.5 1.0 %copy-done.3 = bf16[32,40,69]{2,1,0:T(8,128)(2,1)S(1)} copy-done((bf16[32,40,69]{2,1,0:T(8,128)(2,1)S(1)}, bf16[32,40,69]{2,1,0:T(8,128)(2,1)}, u32[]{:S(2)}) %copy-start.3) | copy-done | bytes 176664
  4.5 52.3 %shard_map.64 = bf16[128,1024]{1,0:T(8,128)(2,1)S(1)} custom-call(bf16[32,40,69]{2,1,0:T(8,128)(2,1)S(1)} %copy-done.3, bf16[9,128,256]{2,1,0:T(8,128)(2,1)S(1)} %pad.4.k1_ref, bf16[3,3,256,256]{3,2,1,0:T(8,128)(2,1)S(1)} %copy-done.1, bf16[256,1024]{1,0:T(8,128)(2,1)S(1)} %copy-done.2), custom_call_target="tpu_custom_call" | custom-call | tf_op jit(solution)/shard_map/pallas_call | solution.py:384
  56.8 0.2 copy.22
  57.0 0.1 bitcast_reduce_fusion
  57.1 0.2 multiply_reduce_fusion
  57.4 0.2 multiply_convert_fusion
  57.5 0.1 copy.14
  57.6 0.1 convert_element_type.62
  57.7 2.1 %fusion.20 = bf16[80,1024]{1,0:T(8,128)(2,1)S(1)} fusion(bf16[80,1024]{1,0:T(8,128)(2,1)S(1)} %convert_element_type.62, bf16[1024,3,1024]{2,0,1:T(8,128)(2,1)} %param.10), kind=kOutput, calls=%fused_computation.19 | convolution fusion | flops 167854080 | bytes 2424832 | tf_op jit(solution)/shard_map/dot_general | solution.py:441
  59.8 0.2 reshape.96
  60.0 2.1 %fusion.17 = bf16[80,1024]{1,0:T(8,128)(2,1)S(1)} fusion(bf16[80,1024]{1,0:T(8,128)(2,1)S(1)} %convert_element_type.62, bf16[1024,3,1024]{2,0,1:T(8,128)(2,1)} %param.10), kind=kOutput, calls=%fused_computation.18 | convolution fusion | flops 167854080 | bytes 2424832 | tf_op jit(solution)/shard_map/dot_general | solution.py:441
  62.1 2.1 %fusion.14 = bf16[80,1024]{1,0:T(8,128)(2,1)S(1)} fusion(bf16[80,1024]{1,0:T(8,128)(2,1)S(1)} %convert_element_type.62, bf16[1024,3,1024]{2,0,1:T(8,128)(2,1)} %param.10), kind=kOutput, calls=%fused_computation.17 | convolution fusion | flops 167854080 | bytes 2424832 | tf_op jit(solution)/shard_map/dot_general | solution.py:441
  64.2 0.2 reshape.95
  64.4 0.4 fusion.33
  64.8 1.2 %convolution_multiply_fusion = f32[2,16,40,40]{2,3,1,0:T(8,128)} fusion(bf16[2,40,16,64]{3,2,1,0:T(8,128)(2,1)S(1)} %reshape.96, bf16[2,40,16,64]{3,2,1,0:T(8,128)(2,1)S(1)} %reshape.95), kind=kOutput, calls=%fused_computation.11 | convolution fusion | flops 6604800 | bytes 532480 | tf_op jit(solution)/shard_map/rqhd,rkhd->rhqk/dot_general | solution.py:449
  66.0 0.2 reshape.94
  66.2 1.7 %fusion.12 = bf16[2,40,16,64]{3,1,2,0:T(8,128)(2,1)S(1)} fusion(bf16[2,40,16,64]{3,2,1,0:T(8,128)(2,1)S(1)} %reshape.94, f32[2,16,40]{2,1,0:T(8,128)S(1)} %fusion.33, f32[2,16,40,40]{2,3,1,0:T(8,128)} %convolution_multiply_fusion), kind=kOutput, calls=%fused_computation.14 | convolution fusion | flops 6790439 | bytes 537600 | tf_op jit(solution)/shard_map/rhqk,rkhd->rqhd/dot_general | solution.py:453
  68.0 0.2 reshape.97
  68.2 0.2 copy.13
  68.5 0.0 copy-done
  68.5 1.2 %fusion.13 = bf16[80,1024]{1,0:T(8,128)(2,1)} fusion(f32[80,1024]{1,0:T(8,128)S(1)} %reshape.99, bf16[80,1024]{1,0:T(8,128)(2,1)S(1)} %reshape.97, bf16[1024,1024]{1,0:T(8,128)(2,1)S(1)} %copy-done), kind=kOutput, calls=%fused_computation.16 | convolution fusion | flops 167936000 | bytes 2752512 | tf_op jit(solution)/shard_map/dot_general | solution.py:467
  (5 shorter events, 0.1 us)
Async XLA Ops:
  0.0 68.5 %copy-start = (bf16[1024,1024]{1,0:T(8,128)(2,1)S(1)}, bf16[1024,1024]{1,0:T(8,128)(2,1)}, u32[]{:S(2)}) copy-start(bf16[1024,1024]{1,0:T(8,128)(2,1)} %param.11) | copy-start | bytes 6291460
  1.2 1.3 %copy-start.1 = (bf16[3,3,256,256]{3,2,1,0:T(8,128)(2,1)S(1)}, bf16[3,3,256,256]{3,2,1,0:T(8,128)(2,1)}, u32[]{:S(2)}) copy-start(bf16[3,3,256,256]{3,2,1,0:T(8,128)(2,1)} %k2_hbm.1) | copy-start | bytes 3538948
  2.5 1.0 %copy-start.2 = (bf16[256,1024]{1,0:T(8,128)(2,1)S(1)}, bf16[256,1024]{1,0:T(8,128)(2,1)}, u32[]{:S(2)}) copy-start(bf16[256,1024]{1,0:T(8,128)(2,1)} %down.1) | copy-start | bytes 1572868
  3.5 1.0 %copy-start.3 = (bf16[32,40,69]{2,1,0:T(8,128)(2,1)S(1)}, bf16[32,40,69]{2,1,0:T(8,128)(2,1)}, u32[]{:S(2)}) copy-start(bf16[32,40,69]{2,1,0:T(8,128)(2,1)} %fields.1) | copy-start | bytes 529924

commit v3 on v2

v3 whole, which is shorter than its diff:
```python
import functools

import jax
import jax.numpy as jnp
from jax import lax
from jax.experimental import pallas as pl
from jax.experimental.pallas import tpu as pltpu
from jax.sharding import PartitionSpec as P

C = 256
D = 1024
HD = 64
WIDE = 48
LANES = 128
SUBS = 2
MESH = pl.DeviceIdType.MESH


epsilon = 1e-05

SIDES = [(da, db) for da in (-1, 0, 1) for db in (-1, 0, 1) if (da, db) != (0, 0)]


def side_rows(da, db, rows, cols):
    return (2 if da else rows) * (8 if db else cols)


def encode_kernel(
    sizes,
    fields_hbm,
    k1_hbm,
    k2_hbm,
    down,
    band,
    fields,
    k1_ref,
    x3,
    xb,
    f_ref,
    s_ref,
    t_ref,
    pb,
    pr,
    qb,
    qr,
    tok,
    tokpad,
    tb,
    wbuf,
    k2,
    *rest,
):
    groups, lats, lons, rows, cols = sizes
    out_halo, in_halo = rest[:8], rest[8:16]
    (
        local_sem,
        halo_send,
        halo_recv,
        z_send,
        z_recv,
        x_send,
        x_recv,
        p_send,
        p_recv,
        q_send,
        q_recv,
        t_send,
        t_recv,
    ) = rest[16:]
    g, a, b = lax.axis_index("groups"), lax.axis_index("lat"), lax.axis_index("lon")
    part = D // groups
    count = (rows // 4) * (cols // 4)
    depth = 16 * C // lats
    shard = depth // lons
    cnt = count // lons
    cp = -(-cnt // 16) * 16

    fields_copy = pltpu.make_async_copy(fields_hbm, fields, local_sem.at[groups + 1])
    fields_copy.start()
    own_copies = [
        pltpu.make_async_copy(
            down.at[:, pl.ds(h * part, part)], wbuf.at[h, b], local_sem.at[1 + h]
        )
        for h in range(groups)
    ]
    for copy in own_copies:
        copy.start()
    k1_copy = pltpu.make_async_copy(k1_hbm, k1_ref, local_sem.at[groups + 2])
    k1_copy.start()
    k2_copy = pltpu.make_async_copy(k2_hbm, k2, local_sem.at[0])
    k2_copy.start()

    barrier = pltpu.get_barrier_semaphore()

    def greet(i, _):
        gg = i // (lats * lons)
        aa = (i // lons) % lats
        bb = i % lons
        pl.semaphore_signal(barrier, inc=1, device_id=(gg, aa, bb), device_id_type=MESH)
        return 0

    lax.fori_loop(0, groups * lats * lons, greet, 0)

    x3[...] = jnp.zeros(x3.shape, jnp.float32)
    fields_copy.wait()
    x3[4 : 4 + rows, 0:cols, 0 : fields.shape[2]] = fields[...].astype(jnp.float32)
    for n, (da, db) in enumerate(SIDES):
        r0, r1 = {-1: (4, 6), 0: (4, 4 + rows), 1: (2 + rows, 4 + rows)}[da]
        c0, c1 = {-1: (0, 8), 0: (0, cols), 1: (cols - 8, cols)}[db]
        out_halo[n][...] = x3[r0:r1, c0:c1, :].reshape(-1, LANES).astype(jnp.bfloat16)

    pl.semaphore_wait(barrier, groups * lats * lons)

    def halo(n):
        da, db = SIDES[n]
        return pltpu.make_async_remote_copy(
            src_ref=out_halo[n],
            dst_ref=in_halo[n],
            send_sem=halo_send.at[n],
            recv_sem=halo_recv.at[n],
            device_id=(g, jnp.clip(a + da, 0, lats - 1), lax.rem(b + db + lons, lons)),
            device_id_type=MESH,
        )

    def inside(index):
        return jnp.logical_and(index >= 0, index < lats)

    for n, (da, db) in enumerate(SIDES):
        if da == 0:
            halo(n).start()
        else:

            @pl.when(inside(a + da))
            def _():
                halo(n).start()

    piece = shard // SUBS

    def some(h, c, u):
        return wbuf.at[h, c, pl.ds(u * piece, piece)]

    def along(c, u, step):
        return pltpu.make_async_remote_copy(
            src_ref=some(g, c, u),
            dst_ref=some(g, c, u),
            send_sem=z_send.at[c, u, (step + 1) // 2],
            recv_sem=z_recv.at[c, u],
            device_id=(g, a, jnp.clip(b + step, 0, lons - 1)),
            device_id_type=MESH,
        )

    def across(c, u, j, incoming=False):
        gg = lax.rem(g + j, groups)
        h = gg if incoming else g
        return pltpu.make_async_remote_copy(
            src_ref=some(h, c, u),
            dst_ref=some(h, c, u),
            send_sem=x_send.at[c, u, j],
            recv_sem=x_recv.at[h, c, u],
            device_id=(gg, a, b),
            device_id_type=MESH,
        )

    def relay(s):
        for u in range(SUBS):
            for way in (1, -1):
                c = b - way * s

                @pl.when(jnp.logical_and(c >= 0, c < lons))
                def _():
                    if s > 0:
                        along(c, u, way).wait_recv()

                    @pl.when(jnp.logical_and(b + way >= 0, b + way < lons))
                    def _():
                        along(c, u, way).start()

                    if s > 0:
                        for j in range(1, groups):
                            across(c, u, j).start()

    for copy in own_copies:
        copy.wait()
    relay(0)

    lane = lax.broadcasted_iota(jnp.int32, (1, 8, LANES), 1)
    for n, (da, db) in enumerate(SIDES):

        def place(n=n, da=da, db=db):
            halo(n).wait_recv()
            r0, nr = {-1: (4 + rows, 2), 0: (4, rows), 1: (2, 2)}[da]
            value = in_halo[n][...].astype(jnp.float32)
            if db == 0:
                x3[r0 : r0 + nr, 0:cols, :] = value.reshape(nr, cols, LANES)
            else:
                value = value.reshape(nr, 8, LANES)
                if db < 0:
                    value = jnp.where(lane < 2, value, 0.0)
                else:
                    value = jnp.where(lane >= 6, value, 0.0)
                    r0 = r0 - 1
                x3[r0 : r0 + nr, cols : cols + 8, :] = x3[r0 : r0 + nr, cols : cols + 8, :] + value

        if da == 0:
            place()
        else:
            pl.when(inside(a - da))(place)
    xb[...] = x3[...].reshape(-1, LANES).astype(jnp.bfloat16)

    def conv(source, start, size, weights, channels):
        total = [None] * 3
        for dr in range(3):
            window = source[pl.ds(pl.multiple_of(start + dr * WIDE, 16), size), 0:channels]
            for dc in range(3):
                term = jnp.dot(window, weights(dr, dc), preferred_element_type=jnp.float32)
                total[dc] = term if total[dc] is None else total[dc] + term
        whole = pltpu.roll(total[0], 1, 0) + total[1] + pltpu.roll(total[2], size - 1, 0)
        return whole[16 : size - 16]

    f_ref[0:16, :] = jnp.zeros((16, C), jnp.bfloat16)
    tail = (rows + 3) * WIDE
    f_ref[tail + 16 : tail + 32, :] = jnp.zeros((16, C), jnp.bfloat16)
    lo = jnp.where(a == 0, 2 * WIDE - 4, -1)
    hi = jnp.where(a == lats - 1, (rows + 2) * WIDE - 4, tail)

    def first_step(k, _):
        size = 5 * WIDE
        value = jax.nn.gelu(
            conv(xb, (5 * k + 1) * WIDE - 16, size + 32, lambda r, c: k1_ref[r, c], k1_ref.shape[2])
        )
        at = k * size + lax.broadcasted_iota(jnp.int32, (size, C), 0)
        value = jnp.where(jnp.logical_and(at >= lo, at < hi), value, 0.0)
        f_ref[pl.ds(pl.multiple_of(16 + k * size, 16), size), :] = value.astype(jnp.bfloat16)
        return 0

    k1_copy.wait()
    lax.fori_loop(0, (rows + 3) // 5, first_step, 0)
    relay(1)
    k2_copy.wait()

    def second_step(k, _):
        size = 4 * WIDE
        value = jax.nn.gelu(
            conv(f_ref, (4 * k + 1) * WIDE, size + 32, lambda r, c: k2[r, c], C)
        )
        own = f_ref[pl.ds(pl.multiple_of(16 + (4 * k + 2) * WIDE, 16), size), :]
        value = own.astype(jnp.float32) + value
        for h in range(C // LANES):
            s_ref[h, pl.ds(pl.multiple_of(k * size, 16), size), :] = value[
                :, h * LANES : (h + 1) * LANES
            ]
        return 0

    def rows_of(ref, start, size):
        return ref.at[pl.ds(pl.multiple_of(start, 16), size)]

    wide = cols // 4

    def to_k(i, j, incoming=False):
        other = lax.rem(a + j, lats)
        sender = lax.rem(a + lats - j, lats) if incoming else a
        return pltpu.make_async_remote_copy(
            src_ref=rows_of(pb, other * count + 16 * i, 16),
            dst_ref=rows_of(pr, sender * count + 16 * i, 16),
            send_sem=p_send.at[i, j],
            recv_sem=p_recv.at[i, j],
            device_id=(g, other, b),
            device_id_type=MESH,
        )

    chunks = count // 16
    done = 0
    for i in range(chunks):
        until = min(-(-16 * (i + 1) // wide), rows // 4)
        lax.fori_loop(done, until, second_step, 0)
        for t in range(done, until):
            for p in range(4):
                for q in range(4):
                    at = (4 * t + p) * WIDE + q
                    for h in range(C // LANES):
                        to = (4 * p + q) * C + h * LANES
                        t_ref[t * wide : (t + 1) * wide, to : to + LANES] = s_ref[
                            h, pl.ds(at, wide, stride=4), :
                        ]
        done = until
        for c in range(lats):
            pb[c * count + 16 * i : c * count + 16 * (i + 1), :] = t_ref[
                16 * i : 16 * (i + 1), c * depth : (c + 1) * depth
            ].astype(jnp.bfloat16)
        for j in range(1, lats):
            to_k(i, j).start()
    mine = pl.ds(pl.multiple_of(a * count, 16), count)
    pr[mine, :] = pb[mine, :]
    tokpad[...] = jnp.zeros(tokpad.shape, jnp.float32)
    for s in range(2, lons):
        relay(s)
    for i in range(chunks):
        for j in range(1, lats):
            to_k(i, j, True).wait_recv()

    def back(i, j, incoming=False):
        h = lax.rem(g + i, groups)
        other = lax.rem(a + j, lats)
        sender = lax.rem(a + lats - j, lats) if incoming else a
        return pltpu.make_async_remote_copy(
            src_ref=rows_of(qb.at[h], other * count, count),
            dst_ref=rows_of(qr.at[h], sender * count, count),
            send_sem=q_send.at[i, j],
            recv_sem=q_recv.at[h, j],
            device_id=(g, other, b),
            device_id_type=MESH,
        )

    block = min(part, 256)
    for i in range(groups):
        h = lax.rem(g + i, groups)
        if i > 0:
            for s in range(1, lons):
                for way in (1, -1):
                    c = b - way * s

                    @pl.when(jnp.logical_and(c >= 0, c < lons))
                    def _():
                        for u in range(SUBS):
                            across(c, u, i, True).wait_recv()

        for n in range(0, part, block):
            total = None
            for c in range(lons):
                term = jnp.dot(
                    pr[:, c * shard : (c + 1) * shard],
                    wbuf[h, c, :, n : n + block],
                    preferred_element_type=jnp.float32,
                )
                total = term if total is None else total + term
            qb[h, :, n : n + block] = total.astype(jnp.bfloat16)
        for j in range(1, lats):
            back(i, j).start()
        qr[h, mine, :] = qb[h, mine, :]

    def to_rows(i, j, incoming=False):
        h = lax.rem(g + i, groups)
        other = lax.rem(b + j, lons)
        sender = lax.rem(b + lons - j, lons) if incoming else b
        return pltpu.make_async_remote_copy(
            src_ref=rows_of(tb.at[h], other * cp, cp),
            dst_ref=rows_of(band.at[h], sender * cp, cp),
            send_sem=t_send.at[i, j],
            recv_sem=t_recv.at[h, j],
            device_id=(g, a, other),
            device_id_type=MESH,
        )

    own = pl.ds(pl.multiple_of(b * cp, 16), cp)
    for i in range(groups):
        h = lax.rem(g + i, groups)
        for j in range(1, lats):
            back(i, j, True).wait_recv()
        total = qr[h, 0:count, :].astype(jnp.float32)
        for c in range(1, lats):
            total = total + qr[h, c * count : (c + 1) * count, :].astype(jnp.float32)
        tok[...] = total
        for c in range(lons):
            tokpad[c * cp : c * cp + cnt, :] = tok[c * cnt : (c + 1) * cnt, :]
        tb[h, :, :] = tokpad[...].astype(jnp.bfloat16)
        for j in range(1, lons):
            to_rows(i, j).start()
        band[h, own, :] = tb[h, own, :]
    for i in range(groups):
        for j in range(1, lons):
            to_rows(i, j, True).wait_recv()

    for n, (da, db) in enumerate(SIDES):
        if da == 0:
            halo(n).wait_send()
        else:

            @pl.when(inside(a + da))
            def _():
                halo(n).wait_send()

    for s in range(lons):
        for way in (1, -1):
            c = b - way * s

            @pl.when(jnp.logical_and(c >= 0, c < lons))
            def _():
                for u in range(SUBS):

                    @pl.when(jnp.logical_and(b + way >= 0, b + way < lons))
                    def _():
                        along(c, u, way).wait_send()

                    if s > 0:
                        for j in range(1, groups):
                            across(c, u, j).wait_send()

    for j in range(1, lats):
        for i in range(chunks):
            to_k(i, j).wait_send()
        for i in range(groups):
            back(i, j).wait_send()
    for j in range(1, lons):
        for i in range(groups):
            to_rows(i, j).wait_send()


def encode(fields, first_kernel, second_kernel, down_weight):
    groups, lats, lons = (lax.axis_size(name) for name in ("groups", "lat", "lon"))
    rows, cols = fields.shape[0], fields.shape[1]
    count = (rows // 4) * (cols // 4)
    depth = 16 * C // lats
    cnt = count // lons
    cp = -(-cnt // 16) * 16
    halos = [
        pltpu.VMEM((side_rows(da, db, rows, cols), LANES), jnp.bfloat16) for da, db in SIDES
    ]
    dma = pltpu.SemaphoreType.DMA
    vmem = pl.BlockSpec(memory_space=pltpu.VMEM)
    hbm = pl.BlockSpec(memory_space=pltpu.HBM)
    bf16, f32 = jnp.bfloat16, jnp.float32
    return pl.pallas_call(
        functools.partial(encode_kernel, (groups, lats, lons, rows, cols)),
        out_shape=jax.ShapeDtypeStruct((groups, lons * cp, D // groups), bf16),
        in_specs=[hbm] * 4,
        out_specs=vmem,
        scratch_shapes=[
            pltpu.VMEM(fields.shape, bf16),
            pltpu.VMEM(first_kernel.shape, bf16),
            pltpu.VMEM((rows + 7, WIDE, LANES), f32),
            pltpu.VMEM(((rows + 7) * WIDE, LANES), bf16),
            pltpu.VMEM(((rows + 3) * WIDE + 32, C), bf16),
            pltpu.VMEM((C // LANES, rows * WIDE, LANES), f32),
            pltpu.VMEM((count, 16 * C), f32),
            pltpu.VMEM((lats * count, depth), bf16),
            pltpu.VMEM((lats * count, depth), bf16),
            pltpu.VMEM((groups, lats * count, D // groups), bf16),
            pltpu.VMEM((groups, lats * count, D // groups), bf16),
            pltpu.VMEM((count, D // groups), f32),
            pltpu.VMEM((lons * cp, D // groups), f32),
            pltpu.VMEM((groups, lons * cp, D // groups), bf16),
            pltpu.VMEM((groups, lons, depth // lons, D // groups), bf16),
            pltpu.VMEM(second_kernel.shape, bf16),
            *halos,
            *halos,
            dma((3 + groups,)),
            dma((8,)),
            dma((8,)),
            dma((lons, SUBS, 2)),
            dma((lons, SUBS)),
            dma((lons, SUBS, groups)),
            dma((groups, lons, SUBS)),
            dma((count // 16, lats)),
            dma((count // 16, lats)),
            dma((groups, lats)),
            dma((groups, lats)),
            dma((groups, lons)),
            dma((groups, lons)),
        ],
        compiler_params=pltpu.CompilerParams(
            collective_id=0, has_side_effects=True, vmem_limit_bytes=44 * 1024 * 1024
        ),
    )(fields, first_kernel, second_kernel, down_weight)


def attention(band, query_weight, key_weight, value_weight):
    row_count, token_count = (band.shape[0], band.shape[1])
    widened = band.astype(jnp.float32)
    average = jnp.mean(widened, axis=-1, keepdims=True)
    centred = widened - average
    spread = jnp.mean(centred * centred, axis=-1, keepdims=True)
    normed = (
        (centred * lax.rsqrt(spread + epsilon))
        .astype(jnp.bfloat16)
        .reshape(row_count * token_count, -1)
    )
    head_count = query_weight.shape[1] // HD

    def project(weight):
        return (
            jnp.dot(normed, weight, preferred_element_type=jnp.float32)
            .astype(jnp.bfloat16)
            .reshape(row_count, token_count, head_count, HD)
        )

    query = project(query_weight)
    keys = project(key_weight)
    values = project(value_weight)
    scores = jnp.einsum(
        "rqhd,rkhd->rhqk", query, keys, preferred_element_type=jnp.float32
    ) * HD ** (-0.5)
    probs = jax.nn.softmax(scores, axis=-1).astype(jnp.bfloat16)
    mixed = jnp.einsum("rhqk,rkhd->rqhd", probs, values, preferred_element_type=jnp.float32).astype(
        jnp.bfloat16
    )
    return mixed.reshape(row_count * token_count, head_count * HD)


def on_device(fields, first_kernel, second_kernel, down_weight, projections, output_weight):
    lons = lax.axis_size("lon")
    wide = fields.shape[1] // 4
    rows = fields.shape[0] // 4 // lons
    band = encode(fields, first_kernel, second_kernel, down_weight)
    band = jnp.concatenate([band[h] for h in range(band.shape[0])], axis=1)
    band = band.reshape(lons, -1, D)[:, : rows * wide].reshape(lons, rows, wide, D)
    band = band.transpose(1, 0, 2, 3).reshape(rows, lons * wide, D)
    mixed = attention(band, projections[:, 0], projections[:, 1], projections[:, 2])
    summed = band.astype(jnp.float32).reshape(-1, D) + jnp.dot(
        mixed, output_weight, preferred_element_type=jnp.float32
    )
    return summed.astype(jnp.bfloat16).reshape(band.shape)


def solution(mesh):
    placed = (P(("groups", "lat"), "lon", None), P(), P(), P(("lat", "lon"), None), P(), P())
    return jax.shard_map(
        on_device,
        mesh=mesh,
        in_specs=placed,
        out_specs=P(("groups", "lat", "lon"), None, None),
        check_vma=False,
    )
```

time: 70 us -> 64.3 us (0.919)
  the two profiles are of different devices: /device:TPU:1 before, /device:TPU:0 now
where the time goes in v3:
time: 64.3 us; the launch traced here: 63.9 us
  Pallas kernels  46.4 us (72%)
  matrix products  10.7 us (17%)
  local copies, waits for them, and re-layouts  5.96 us (9%)
  other arithmetic  0.74 us (1%)
    pallas_call x1, Pallas kernels, encode(): pl.pallas_call(functools.partial(encode_kernel, (groups, lats, lons, rows...  46.4 us
    dot_general x3, matrix products, project(): jnp.dot(normed, weight, preferred_element_type=jnp.float32)  6.24 us
    unnamed x10, local copies, waits for them, and re-layouts  4.41 us
    dot_general x1, matrix products, attention(): jnp.einsum('rhqk,rkhd->rqhd', probs, values, preferred_element_type=jnp.f...  1.71 us

profile of v3, /device:TPU:0, one launch (start us, length us, event | category | flops | bytes accessed | tf_op | source)
XLA Modules:
  0.0 63.9 jit_solution(11056073868319763777)
XLA Ops:
  0.0 0.0 copy-start
  0.0 0.0 copy-start.1
  0.0 1.4 %copy-done.1 = bf16[3,3,256,256]{3,2,1,0:T(8,128)(2,1)S(1)} copy-done((bf16[3,3,256,256]{3,2,1,0:T(8,128)(2,1)S(1)}, bf16[3,3,256,256]{3,2,1,0:T(8,128)(2,1)}, u32[]{:S(2)}) %copy-start.1) | copy-done | bytes 1179672
  1.4 0.0 copy-start.2
  1.4 1.0 %copy-done.2 = bf16[256,1024]{1,0:T(8,128)(2,1)S(1)} copy-done((bf16[256,1024]{1,0:T(8,128)(2,1)S(1)}, bf16[256,1024]{1,0:T(8,128)(2,1)}, u32[]{:S(2)}) %copy-start.2) | copy-done | bytes 524312
  2.5 0.0 copy-start.3
  2.5 1.0 %copy-done.3 = bf16[3,3,69,256]{3,2,1,0:T(8,128)(2,1)S(1)} copy-done((bf16[3,3,69,256]{3,2,1,0:T(8,128)(2,1)S(1)}, bf16[3,3,69,256]{3,2,1,0:T(8,128)(2,1)}, u32[]{:S(2)}) %copy-start.3) | copy-done | bytes 317976
  3.4 0.0 copy-start.4
  3.4 1.0 %copy-done.4 = bf16[32,40,69]{2,1,0:T(8,128)(2,1)S(1)} copy-done((bf16[32,40,69]{2,1,0:T(8,128)(2,1)S(1)}, bf16[32,40,69]{2,1,0:T(8,128)(2,1)}, u32[]{:S(2)}) %copy-start.4) | copy-done | bytes 176664
  4.4 46.4 %shard_map.64 = bf16[2,128,512]{2,1,0:T(8,128)(2,1)S(1)} custom-call(bf16[32,40,69]{2,1,0:T(8,128)(2,1)S(1)} %copy-done.4, bf16[3,3,69,256]{3,2,1,0:T(8,128)(2,1)S(1)} %copy-done.3, bf16[3,3,256,256]{3,2,1,0:T(8,128)(2,1)S(1)} %copy-done.1, bf16[256,1024]{1,0:T(8,128)(2,1)S(1)} %copy-done.2), custom_call_target="tpu_custom_call" | custom-call | tf_op jit(solution)/shard_map/pallas_call | solution.py:422
  50.9 0.1 copy.12
  51.0 0.1 copy.13
  51.1 0.1 pad_maximum_fusion
  51.2 0.1 fusion.27
  51.3 0.2 multiply_reduce_fusion
  51.6 0.2 multiply_convert_fusion
  51.8 0.1 copy.15
  51.9 0.1 convert_element_type.60
  52.0 2.1 %fusion.20 = bf16[80,1024]{1,0:T(8,128)(2,1)S(1)} fusion(bf16[80,1024]{1,0:T(8,128)(2,1)S(1)} %convert_element_type.60, bf16[1024,3,1024]{2,0,1:T(8,128)(2,1)} %param.10), kind=kOutput, calls=%fused_computation.19 | convolution fusion | flops 167854080 | bytes 2424832 | tf_op jit(solution)/shard_map/dot_general | solution.py:481
  54.0 0.2 reshape.93
  54.3 2.1 %fusion.17 = bf16[80,1024]{1,0:T(8,128)(2,1)S(1)} fusion(bf16[80,1024]{1,0:T(8,128)(2,1)S(1)} %convert_element_type.60, bf16[1024,3,1024]{2,0,1:T(8,128)(2,1)} %param.10), kind=kOutput, calls=%fused_computation.18 | convolution fusion | flops 167854080 | bytes 2424832 | tf_op jit(solution)/shard_map/dot_general | solution.py:481
  56.4 2.1 %fusion.14 = bf16[80,1024]{1,0:T(8,128)(2,1)S(1)} fusion(bf16[80,1024]{1,0:T(8,128)(2,1)S(1)} %convert_element_type.60, bf16[1024,3,1024]{2,0,1:T(8,128)(2,1)} %param.10), kind=kOutput, calls=%fused_computation.17 | convolution fusion | flops 167854080 | bytes 2424832 | tf_op jit(solution)/shard_map/dot_general | solution.py:481
  58.4 0.2 reshape.92
  58.7 0.4 fusion.35
  59.1 1.2 %convolution_multiply_fusion = f32[2,16,40,40]{2,3,1,0:T(8,128)} fusion(bf16[2,40,16,64]{3,2,1,0:T(8,128)(2,1)S(1)} %reshape.93, bf16[2,40,16,64]{3,2,1,0:T(8,128)(2,1)S(1)} %reshape.92), kind=kOutput, calls=%fused_computation.11 | convolution fusion | flops 6604800 | bytes 532480 | tf_op jit(solution)/shard_map/rqhd,rkhd->rhqk/dot_general | solution.py:489
  60.2 0.2 reshape.91
  60.5 1.7 %fusion.12 = bf16[2,40,16,64]{3,1,2,0:T(8,128)(2,1)S(1)} fusion(bf16[2,40,16,64]{3,2,1,0:T(8,128)(2,1)S(1)} %reshape.91, f32[2,16,40]{2,1,0:T(8,128)S(1)} %fusion.35, f32[2,16,40,40]{2,3,1,0:T(8,128)} %convolution_multiply_fusion), kind=kOutput, calls=%fused_computation.14 | convolution fusion | flops 6790439 | bytes 537600 | tf_op jit(solution)/shard_map/rhqk,rkhd->rqhd/dot_general | solution.py:493
  62.2 0.2 reshape.94
  62.5 0.2 copy.14
  62.8 0.0 copy-done
  62.8 1.2 %fusion.13 = bf16[80,1024]{1,0:T(8,128)(2,1)} fusion(f32[80,1024]{1,0:T(8,128)S(1)} %reshape.96, bf16[80,1024]{1,0:T(8,128)(2,1)S(1)} %reshape.94, bf16[1024,1024]{1,0:T(8,128)(2,1)S(1)} %copy-done), kind=kOutput, calls=%fused_computation.16 | convolution fusion | flops 167936000 | bytes 2752512 | tf_op jit(solution)/shard_map/dot_general | solution.py:508
  (6 shorter events, 0.2 us)
Async XLA Ops:
  0.0 62.8 %copy-start = (bf16[1024,1024]{1,0:T(8,128)(2,1)S(1)}, bf16[1024,1024]{1,0:T(8,128)(2,1)}, u32[]{:S(2)}) copy-start(bf16[1024,1024]{1,0:T(8,128)(2,1)} %param.11) | copy-start | bytes 6291460
  0.0 1.4 %copy-start.1 = (bf16[3,3,256,256]{3,2,1,0:T(8,128)(2,1)S(1)}, bf16[3,3,256,256]{3,2,1,0:T(8,128)(2,1)}, u32[]{:S(2)}) copy-start(bf16[3,3,256,256]{3,2,1,0:T(8,128)(2,1)} %k2_hbm.1) | copy-start | bytes 3538948
  1.4 1.0 %copy-start.2 = (bf16[256,1024]{1,0:T(8,128)(2,1)S(1)}, bf16[256,1024]{1,0:T(8,128)(2,1)}, u32[]{:S(2)}) copy-start(bf16[256,1024]{1,0:T(8,128)(2,1)} %down.1) | copy-start | bytes 1572868
  2.5 1.0 %copy-start.3 = (bf16[3,3,69,256]{3,2,1,0:T(8,128)(2,1)S(1)}, bf16[3,3,69,256]{3,2,1,0:T(8,128)(2,1)}, u32[]{:S(2)}) copy-start(bf16[3,3,69,256]{3,2,1,0:T(8,128)(2,1)} %k1_hbm.1) | copy-start | bytes 953860
  3.4 1.0 %copy-start.4 = (bf16[32,40,69]{2,1,0:T(8,128)(2,1)S(1)}, bf16[32,40,69]{2,1,0:T(8,128)(2,1)}, u32[]{:S(2)}) copy-start(bf16[32,40,69]{2,1,0:T(8,128)(2,1)} %fields_hbm.1) | copy-start | bytes 529924

commit v4 on v3

--- a/solution.py
+++ b/solution.py
@@ -13,6 +13,7 @@
 WIDE = 48
 LANES = 128
 SUBS = 2
+VMEM_BYTES = 62 * 1024 * 1024
 MESH = pl.DeviceIdType.MESH
 
 
@@ -92,14 +93,18 @@
 
     barrier = pltpu.get_barrier_semaphore()
 
-    def greet(i, _):
-        gg = i // (lats * lons)
-        aa = (i // lons) % lats
-        bb = i % lons
-        pl.semaphore_signal(barrier, inc=1, device_id=(gg, aa, bb), device_id_type=MESH)
-        return 0
-
-    lax.fori_loop(0, groups * lats * lons, greet, 0)
+    def greet(device):
+        pl.semaphore_signal(barrier, inc=1, device_id=device, device_id_type=MESH)
+
+    for j in range(1, lats):
+        greet((g, lax.rem(a + j, lats), b))
+    for j in range(1, lons):
+        greet((g, a, lax.rem(b + j, lons)))
+    for j in range(1, groups):
+        greet((lax.rem(g + j, groups), a, b))
+    for da in (-1, 1):
+        for db in (-1, 1):
+            greet((g, lax.rem(a + da + lats, lats), lax.rem(b + db + lons, lons)))
 
     x3[...] = jnp.zeros(x3.shape, jnp.float32)
     fields_copy.wait()
@@ -109,7 +114,7 @@
         c0, c1 = {-1: (0, 8), 0: (0, cols), 1: (cols - 8, cols)}[db]
         out_halo[n][...] = x3[r0:r1, c0:c1, :].reshape(-1, LANES).astype(jnp.bfloat16)
 
-    pl.semaphore_wait(barrier, groups * lats * lons)
+    pl.semaphore_wait(barrier, lats + lons + groups + 1)
 
     def halo(n):
         da, db = SIDES[n]
@@ -458,12 +463,12 @@
             dma((groups, lons)),
         ],
         compiler_params=pltpu.CompilerParams(
-            collective_id=0, has_side_effects=True, vmem_limit_bytes=44 * 1024 * 1024
+            collective_id=0, has_side_effects=True, vmem_limit_bytes=VMEM_BYTES
         ),
     )(fields, first_kernel, second_kernel, down_weight)
 
 
-def attention(band, query_weight, key_weight, value_weight):
+def project_all(band, query_weight, key_weight, value_weight):
     row_count, token_count = (band.shape[0], band.shape[1])
     widened = band.astype(jnp.float32)
     average = jnp.mean(widened, axis=-1, keepdims=True)
@@ -474,26 +479,41 @@
         .astype(jnp.bfloat16)
         .reshape(row_count * token_count, -1)
     )
-    head_count = query_weight.shape[1] // HD
-
     def project(weight):
-        return (
-            jnp.dot(normed, weight, preferred_element_type=jnp.float32)
-            .astype(jnp.bfloat16)
-            .reshape(row_count, token_count, head_count, HD)
-        )
-
-    query = project(query_weight)
-    keys = project(key_weight)
-    values = project(value_weight)
-    scores = jnp.einsum(
-        "rqhd,rkhd->rhqk", query, keys, preferred_element_type=jnp.float32
-    ) * HD ** (-0.5)
-    probs = jax.nn.softmax(scores, axis=-1).astype(jnp.bfloat16)
-    mixed = jnp.einsum("rhqk,rkhd->rqhd", probs, values, preferred_element_type=jnp.float32).astype(
-        jnp.bfloat16
-    )
-    return mixed.reshape(row_count * token_count, head_count * HD)
+        return jnp.dot(normed, weight, preferred_element_type=jnp.float32).astype(jnp.bfloat16)
+
+    return project(query_weight), project(key_weight), project(value_weight)
+
+
+def mix_kernel(keys_in_row, query, keys, values, band, output_weight, out, mixed):
+    count = query.shape[0]
+    at = [lax.broadcasted_iota(jnp.int32, (count, count), dim) for dim in (0, 1)]
+    same = None
+    for r in range(count // keys_in_row):
+        lo, hi = r * keys_in_row, (r + 1) * keys_in_row
+        both = (at[0] >= lo) & (at[0] < hi) & (at[1] >= lo) & (at[1] < hi)
+        same = both if same is None else same | both
+    for n in range(query.shape[1] // HD):
+        head = slice(n * HD, (n + 1) * HD)
+        scores = lax.dot_general(
+            query[:, head],
+            keys[:, head],
+            (((1,), (1,)), ((), ())),
+            preferred_element_type=jnp.float32,
+        ) * HD ** (-0.5)
+        scores = jnp.where(same, scores, -jnp.inf)
+        powers = jnp.exp(scores - jnp.max(scores, axis=-1, keepdims=True))
+        probs = (powers / jnp.sum(powers, axis=-1, keepdims=True)).astype(jnp.bfloat16)
+        mixed[:, head] = jnp.dot(
+            probs, values[:, head], preferred_element_type=jnp.float32
+        ).astype(jnp.bfloat16)
+    for n in range(0, D, 256):
+        out[:, n : n + 256] = (
+            band[:, n : n + 256].astype(jnp.float32)
+            + jnp.dot(
+                mixed[...], output_weight[:, n : n + 256], preferred_element_type=jnp.float32
+            )
+        ).astype(jnp.bfloat16)
 
 
 def on_device(fields, first_kernel, second_kernel, down_weight, projections, output_weight):
@@ -504,11 +524,19 @@
     band = jnp.concatenate([band[h] for h in range(band.shape[0])], axis=1)
     band = band.reshape(lons, -1, D)[:, : rows * wide].reshape(lons, rows, wide, D)
     band = band.transpose(1, 0, 2, 3).reshape(rows, lons * wide, D)
-    mixed = attention(band, projections[:, 0], projections[:, 1], projections[:, 2])
-    summed = band.astype(jnp.float32).reshape(-1, D) + jnp.dot(
-        mixed, output_weight, preferred_element_type=jnp.float32
+    query, keys, values = project_all(
+        band, projections[:, 0], projections[:, 1], projections[:, 2]
     )
-    return summed.astype(jnp.bfloat16).reshape(band.shape)
+    flat = band.reshape(-1, D)
+    latent = pl.pallas_call(
+        functools.partial(mix_kernel, lons * wide),
+        out_shape=jax.ShapeDtypeStruct(flat.shape, jnp.bfloat16),
+        in_specs=[pl.BlockSpec(memory_space=pltpu.VMEM)] * 5,
+        out_specs=pl.BlockSpec(memory_space=pltpu.VMEM),
+        scratch_shapes=[pltpu.VMEM(flat.shape, jnp.bfloat16)],
+        compiler_params=pltpu.CompilerParams(vmem_limit_bytes=16 * 1024 * 1024),
+    )(query, keys, values, flat, output_weight)
+    return latent.reshape(band.shape)
 
 
 def solution(mesh):

time: 64.3 us -> 57.3 us (0.89)
  local copies, waits for them, and re-layouts: 5.96 us -> 1.44 us
  matrix products: 10.7 us -> 6.39 us
  Pallas kernels: 46.4 us -> 48.4 us
    unnamed x10 -> x2, local copies, waits for them, and re-layouts: 4.41 us -> 0.01 us
    dot_general x3 -> x0, matrix products: 4.03 us -> none  [the longest x1 1.71 us: attention(): jnp.einsum('rhqk,rkhd->rqhd', probs, values, preferred_element_type=jnp.f...]
    pallas_call x0 -> x1, Pallas kernels: none -> 2.7 us  [on_device(): pl.pallas_call(functools.partial(mix_kernel, lons * wide), out_shape=jax....]
    slice x1, local copies, waits for them, and re-layouts: 0.02 us -> 0.99 us  [on_device(): band = jnp.concatenate([band[h] for h in range(band.shape[0])], axis=1)]
    reshape x4 -> x0, local copies, waits for them, and re-layouts: 0.92 us -> none  [the longest x3 0.69 us: project(): return jnp.dot(normed, weight, preferred_element_type=jnp.float32).astype...]
    pallas_call x1, Pallas kernels: 46.4 us -> 45.8 us  [encode(): pl.pallas_call(functools.partial(encode_kernel, (groups, lats, lons, rows...]
where the time goes in v4:
time: 57.3 us; the launch traced here: 57.1 us
  Pallas kernels  48.4 us (84%)
  matrix products  6.39 us (11%)
  local copies, waits for them, and re-layouts  1.44 us (3%)
  other arithmetic  0.71 us (1%)
    pallas_call x1, Pallas kernels, encode(): pl.pallas_call(functools.partial(encode_kernel, (groups, lats, lons, rows...  45.8 us
    dot_general x3, matrix products, project(): jnp.dot(normed, weight, preferred_element_type=jnp.float32)  6.39 us
    pallas_call x1, Pallas kernels, on_device(): pl.pallas_call(functools.partial(mix_kernel, lons * wide), out_shape=jax....  2.7 us

profile of v4, /device:TPU:0, one launch (start us, length us, event | category | flops | bytes accessed | tf_op | source)
XLA Modules:
  0.0 57.1 jit_solution(17343753369965325505)
XLA Ops:
  0.0 45.8 %shard_map.64 = bf16[2,128,512]{2,1,0:T(8,128)(2,1)} custom-call(bf16[32,40,69]{2,1,0:T(8,128)(2,1)} %fields_hbm.1, bf16[3,3,69,256]{3,2,1,0:T(8,128)(2,1)} %k1_hbm.1, bf16[3,3,256,256]{3,2,1,0:T(8,128)(2,1)} %k2_hbm.1, bf16[256,1024]{1,0:T(8,128)(2,1)} %down.1), custom_call_target="tpu_custom_call" | custom-call | tf_op jit(solution)/shard_map/pallas_call | solution.py:427
  45.8 1.0 %fusion.22 = (bf16[1,128,512]{2,1,0:T(8,128)(2,1)S(1)}, bf16[1,128,512]{2,1,0:T(8,128)(2,1)S(1)}) fusion(bf16[2,128,512]{2,1,0:T(8,128)(2,1)} %shard_map.64), kind=kLoop, calls=%fused_computation.21 | loop fusion | bytes 524288 | tf_op jit(solution)/shard_map/slice | solution.py:524
  46.8 0.1 copy.7
  46.9 0.1 copy.8
  47.0 0.1 pad_maximum_fusion
  47.1 0.1 convert_reduce_fusion
  47.2 0.2 fusion.20
  47.5 0.2 fusion.21
  47.7 0.1 copy.10
  47.8 0.1 reshape_reshape.3.band
  47.8 0.1 copy.9
  47.9 0.1 convert_element_type.29
  48.0 2.1 %fusion.15.values = bf16[80,1024]{1,0:T(8,128)(2,1)S(1)} fusion(bf16[80,1024]{1,0:T(8,128)(2,1)S(1)} %convert_element_type.29, bf16[1024,3,1024]{2,0,1:T(8,128)(2,1)} %param.10), kind=kOutput, calls=%fused_computation.11 | convolution fusion | flops 167854080 | bytes 2424832 | tf_op jit(solution)/shard_map/dot_general | solution.py:483
  50.1 0.0 copy-start
  50.1 2.2 %fusion.12.keys = bf16[80,1024]{1,0:T(8,128)(2,1)S(1)} fusion(bf16[80,1024]{1,0:T(8,128)(2,1)S(1)} %convert_element_type.29, bf16[1024,3,1024]{2,0,1:T(8,128)(2,1)} %param.10), kind=kOutput, calls=%fused_computation.10 | convolution fusion | flops 167854080 | bytes 2424832 | tf_op jit(solution)/shard_map/dot_general | solution.py:483
  52.3 2.1 %fusion.9.query = bf16[80,1024]{1,0:T(8,128)(2,1)S(1)} fusion(bf16[80,1024]{1,0:T(8,128)(2,1)S(1)} %convert_element_type.29, bf16[1024,3,1024]{2,0,1:T(8,128)(2,1)} %param.10), kind=kOutput, calls=%fused_computation.9 | convolution fusion | flops 167854080 | bytes 2424832 | tf_op jit(solution)/shard_map/dot_general | solution.py:483
  54.4 0.0 copy-done
  54.4 2.7 %shard_map.65 = bf16[80,1024]{1,0:T(8,128)(2,1)} custom-call(bf16[80,1024]{1,0:T(8,128)(2,1)S(1)} %fusion.9.query, bf16[80,1024]{1,0:T(8,128)(2,1)S(1)} %fusion.12.keys, bf16[80,1024]{1,0:T(8,128)(2,1)S(1)} %fusion.15.values, bf16[80,1024]{1,0:T(8,128)(2,1)S(1)} %reshape_reshape.3.band, bf16[1024,1024]{1,0:T(8,128)(2,1)S(1)} %copy-done), custom_call_target="tpu_custom_call" | custom-call | tf_op jit(solution)/shard_map/pallas_call | solution.py:531
  (2 shorter events, 0.0 us)
Async XLA Ops:
  50.1 4.3 %copy-start = (bf16[1024,1024]{1,0:T(8,128)(2,1)S(1)}, bf16[1024,1024]{1,0:T(8,128)(2,1)}, u32[]{:S(2)}) copy-start(bf16[1024,1024]{1,0:T(8,128)(2,1)} %output_weight.1) | copy-start | bytes 6291460
